TPU v7x, 128 devices: a whole 4x4x4 slice. The times are simulated.
128 devices in a mesh: shot: 8 (over x, z_lo), dom: 16 (over z_hi, y, core).
Axes of the slice: x: 4, y: 4, z: 4 (z_hi: 2, z_lo: 2; z = z_hi * 2 + z_lo), core: 2. Of those that a mesh axis runs over, the one named last changes fastest.
Arguments:
- velocity: float32 [16, 16, 4, 64, 512], P('shot', 'dom'), may hold values from 0.05 to 0.18
- fwd_prev: float32 [8, 64, 64, 512], P('shot', 'dom'), may hold values from -3 to 3
- fwd_cur: float32 [8, 64, 64, 512], P('shot', 'dom'), may hold values from -3 to 3
- adj_prev: float32 [8, 64, 64, 512], P('shot', 'dom'), may hold values from -3 to 3
- adj_cur: float32 [8, 64, 64, 512], P('shot', 'dom'), may hold values from -3 to 3
- wavelet: float32 [8, 8], P('shot'), may hold values from -24 to 24
- src_pos: int32 [8], P('shot'), may hold values from 0 to 2097151
- rec_pos: int32 [8, 256], P('shot'), may hold values from 0 to 2097151
- observed: float32 [8, 8, 256], P('shot'), may hold values from -6 to 6
- step_count: int32 [8], P('shot'), may hold values from 4 to 8
- aperture: int32 [8, 16], replicated, may hold values from 0 to 255, as said below
- block_slot: int32 [16], replicated, may hold values from 0 to 15, each once
- prev_batch: float32 [16, 16, 4, 64, 512], P('shot', 'dom'), may hold values from -6 to 6
- snapshot: float32 [16, 16, 4, 64, 512], P('shot', 'dom'), may hold values from -6 to 6
Outputs:
- reduced_grad: float32 [16, 16, 4, 64, 512], P('shot', 'dom')
Inputs may be any that keep to these rules, and one draw needn't show every extreme that they name: `aperture`: row s is (b0 + k) * 8 + y for k = 0 .. 15, with b0 in 0 .. 16 and y in 0 .. 7 taken per row.
All inputs are finite; a program needn't handle non-finite values.
Results may differ from a plain program's by a relative error of at most 0.0003.
Values sent between devices are 32-bit elements; how exact they have to be, the bound alone decides.
A program may use at most 128 MiB of HBM per device.

v0:
```python
import jax
import jax.numpy as jnp
from jax import lax
from jax.sharding import PartitionSpec as P

COEFS = (-205.0 / 72.0, 8.0 / 5.0, -1.0 / 5.0, 8.0 / 315.0, -1.0 / 560.0)


def padded_2(cells, sides, width):
    for axis, dim in sides:
        count = lax.axis_size(axis)
        ends = count - 1
        head = lax.slice_in_dim(cells, 0, width, axis=dim)
        tail = lax.slice_in_dim(cells, cells.shape[dim] - width, cells.shape[dim], axis=dim)
        cells = jnp.concatenate(
            [
                lax.ppermute(tail, axis, [(i, (i + 1) % count) for i in range(ends)]),
                cells,
                lax.ppermute(head, axis, [((i + 1) % count, i) for i in range(ends)]),
            ],
            axis=dim,
        )
    return cells


def stencil(padded):
    size_x = padded.shape[0] - 8
    size_y = padded.shape[1] - 8
    size_z = padded.shape[2] - 8
    center = padded[4 : 4 + size_x, 4 : 4 + size_y, 4 : 4 + size_z]
    total = 3.0 * COEFS[0] * center
    for reach in range(1, 5):
        along_x = (
            padded[4 + reach : 4 + reach + size_x, 4 : 4 + size_y, 4 : 4 + size_z]
            + padded[4 - reach : 4 - reach + size_x, 4 : 4 + size_y, 4 : 4 + size_z]
        )
        along_y = (
            padded[4 : 4 + size_x, 4 + reach : 4 + reach + size_y, 4 : 4 + size_z]
            + padded[4 : 4 + size_x, 4 - reach : 4 - reach + size_y, 4 : 4 + size_z]
        )
        along_z = (
            padded[4 : 4 + size_x, 4 : 4 + size_y, 4 + reach : 4 + reach + size_z]
            + padded[4 : 4 + size_x, 4 : 4 + size_y, 4 - reach : 4 - reach + size_z]
        )
        total = total + COEFS[reach] * (along_x + along_y + along_z)
    return total


def laplacian(field):
    padded = padded_2(field, (("dom", 0),), 4)
    padded = jnp.pad(padded, ((0, 0), (4, 4), (4, 4)))
    return stencil(padded)


def local(
    velocity,
    fwd_prev,
    fwd_cur,
    adj_prev,
    adj_cur,
    wavelet,
    src_pos,
    rec_pos,
    observed,
    step_count,
    aperture,
    block_slot,
    prev_batch,
    snapshot,
):
    shots = lax.axis_size("shot")
    columns = lax.axis_size("dom")
    shot_id = lax.axis_index("shot")
    column = lax.axis_index("dom")
    blk_dev = velocity.shape[0]
    cells = velocity.shape[2:]
    slab_cells = cells[0] * cells[1] * cells[2]
    row_count = blk_dev * shots // 2
    starts = aperture[:, 0] // row_count
    turns = starts % columns
    position = (column - turns) % columns
    needed = jnp.take_along_axis(aperture, position[:, None], axis=1)[:, 0]
    needed_x = needed // row_count
    needed_y = needed % row_count
    slots_all = block_slot[needed_x // columns * row_count + needed_y]
    my_slot = slots_all[shot_id]
    my_turn = turns[shot_id]
    share = velocity.reshape((blk_dev,) + cells)
    piece = lax.all_gather(share, "shot", axis=0, tiled=True)
    start = jnp.int32(0)
    count = piece.shape[0]
    offset = jnp.clip(my_slot, 0, count - 1)
    row = lax.dynamic_index_in_dim(piece, offset, 0, keepdims=False)
    inside = (my_slot >= start) & (my_slot < start + count)
    local_pick = jnp.where(inside, row, 0.0)
    everyone = lax.all_gather(local_pick[None], "dom", axis=0, tiled=True)
    slab = lax.dynamic_index_in_dim(everyone, (column + my_turn) % columns, 0, keepdims=False)
    base = column * slab_cells
    src_local = src_pos[0] - base
    src_inside = (src_local >= 0) & (src_local < slab_cells)
    src_index = jnp.clip(src_local, 0, slab_cells - 1)
    rec_local = rec_pos[0] - base
    rec_inside = (rec_local >= 0) & (rec_local < slab_cells)
    rec_index = jnp.clip(rec_local, 0, slab_cells - 1)
    count = step_count[0]
    total_steps = wavelet.shape[1]
    u_prev = fwd_prev[0]
    u_cur = fwd_cur[0]
    laps = []
    samples = []
    for step in range(total_steps):
        active = step < count
        lap = laplacian(u_cur)
        u_next = 2.0 * u_cur - u_prev + slab * lap
        u_next = (
            u_next.reshape(-1)
            .at[src_index]
            .add(jnp.where(src_inside, wavelet[0, step], 0.0))
            .reshape(cells)
        )
        u_prev, u_cur = (jnp.where(active, u_cur, u_prev), jnp.where(active, u_next, u_cur))
        laps.append(lap)
        samples.append(u_cur.reshape(-1)[rec_index])
    p_prev = adj_prev[0]
    p_cur = adj_cur[0]
    grad = jnp.zeros(cells, jnp.float32)
    for step in reversed(range(total_steps)):
        active = step < count
        residual = jnp.where(rec_inside & active, samples[step] - observed[0, step], 0.0)
        p_hit = p_cur.reshape(-1).at[rec_index].add(residual).reshape(cells)
        grad = grad + jnp.where(active, p_hit * laps[step], 0.0)
        p_next = 2.0 * p_hit - p_prev + laplacian(slab * p_hit)
        p_prev, p_cur = (jnp.where(active, p_hit, p_prev), jnp.where(active, p_next, p_cur))
    every_grad = lax.all_gather(grad[None], "dom", axis=0, tiled=True)
    grad_col = lax.dynamic_index_in_dim(every_grad, (column - my_turn) % columns, 0, keepdims=False)
    wanted = jnp.arange(lax.axis_size("shot") * blk_dev, dtype=jnp.int32)
    inside = wanted == my_slot
    batch = lax.psum_scatter(
        jnp.where(inside[:, None, None, None], grad_col[None], 0.0),
        "shot",
        scatter_dimension=0,
        tiled=True,
    )
    result = batch - prev_batch.reshape(batch.shape) + snapshot.reshape(batch.shape)
    return result.reshape(velocity.shape)


def solution(mesh):
    placed = (
        P("shot", "dom", None, None, None),
        P("shot", "dom", None, None),
        P("shot", "dom", None, None),
        P("shot", "dom", None, None),
        P("shot", "dom", None, None),
        P("shot", None),
        P("shot"),
        P("shot", None),
        P("shot", None, None),
        P("shot"),
        P(),
        P(),
        P("shot", "dom", None, None, None),
        P("shot", "dom", None, None, None),
    )
    return jax.shard_map(
        local,
        mesh=mesh,
        in_specs=placed,
        out_specs=P("shot", "dom", None, None, None),
        check_vma=False,
    )
```

profile of v0, /device:TPU:0, one launch (start us, length us, event | category | flops | bytes accessed | tf_op | source)
XLA Modules:
  0.0 915.0 jit_solution(5534974857815732719)
XLA Ops:
  12.8 167.1 %all-gather.7.cloned.1.call-done = f32[16,1,4,64,512]{4,3,2,1,0:T(8,128)} async-done(((f32[2,1,4,64,512]{4,3,2,1,0:T(8,128)}), f32[16,1,4,64,512]{4,3,2,1,0:T(8,128)}) %all-gather.7.cloned.1.call-update) | async-done | bytes 8388624 | tf_op jit(solution)/shard_map/all_gather | solution.py:89
  192.6 70.6 %all-gather.11.cloned.1.call-done = f32[16,1,4,64,512]{4,3,2,1,0:T(8,128)} async-done(((f32[1,1,4,64,512]{4,3,2,1,0:T(8,128)}), f32[16,1,4,64,512]{4,3,2,1,0:T(8,128)}) %all-gather.11.cloned.1.call-update) | async-done | bytes 8388624 | tf_op jit(solution)/shard_map/all_gather | solution.py:96
  263.2 4.6 fusion.363
  275.8 4.5 fusion.364
  284.0 9.5 %collective-permute-start.5 = (f32[4,64,512]{2,1,0:T(8,128)S(1)}, f32[4,64,512]{2,1,0:T(8,128)}, u32[]{:S(2)}, u32[]{:S(2)}) collective-permute-start(f32[4,64,512]{2,1,0:T(8,128)S(1)} %broadcast_select_fusion.10), channel_id=1, source_target_pairs={{0,1},{1,2},{2,3},{3,4},{4,5},{5,6},{6,7},{7,8},{8,9},{9,10},{10,1... | collective-permute-start | bytes 1572872 | tf_op jit(solution)/shard_map/ppermute | solution.py:17
  296.3 4.9 fusion.365
  305.0 10.7 %collective-permute-start.7 = (f32[4,64,512]{2,1,0:T(8,128)S(1)}, f32[4,64,512]{2,1,0:T(8,128)}, u32[]{:S(2)}, u32[]{:S(2)}) collective-permute-start(f32[4,64,512]{2,1,0:T(8,128)S(1)} %broadcast_select_fusion.12), channel_id=1, source_target_pairs={{0,1},{1,2},{2,3},{3,4},{4,5},{5,6},{6,7},{7,8},{8,9},{9,10},{10,1... | collective-permute-start | bytes 1572872 | tf_op jit(solution)/shard_map/ppermute | solution.py:17
  318.3 5.1 fusion.366
  327.1 10.0 %collective-permute-start.9 = (f32[4,64,512]{2,1,0:T(8,128)S(1)}, f32[4,64,512]{2,1,0:T(8,128)}, u32[]{:S(2)}, u32[]{:S(2)}) collective-permute-start(f32[4,64,512]{2,1,0:T(8,128)S(1)} %broadcast_select_fusion.15), channel_id=1, source_target_pairs={{0,1},{1,2},{2,3},{3,4},{4,5},{5,6},{6,7},{7,8},{8,9},{9,10},{10,1... | collective-permute-start | bytes 1572872 | tf_op jit(solution)/shard_map/ppermute | solution.py:17
  339.9 5.1 fusion.367
  348.8 10.5 %collective-permute-start.11 = (f32[4,64,512]{2,1,0:T(8,128)S(1)}, f32[4,64,512]{2,1,0:T(8,128)}, u32[]{:S(2)}, u32[]{:S(2)}) collective-permute-start(f32[4,64,512]{2,1,0:T(8,128)S(1)} %broadcast_select_fusion.18), channel_id=1, source_target_pairs={{0,1},{1,2},{2,3},{3,4},{4,5},{5,6},{6,7},{7,8},{8,9},{9,10},{10,1... | collective-permute-start | bytes 1572872 | tf_op jit(solution)/shard_map/ppermute | solution.py:17
  362.0 5.3 fusion.368
  370.0 10.5 %collective-permute-start.13 = (f32[4,64,512]{2,1,0:T(8,128)S(1)}, f32[4,64,512]{2,1,0:T(8,128)}, u32[]{:S(2)}, u32[]{:S(2)}) collective-permute-start(f32[4,64,512]{2,1,0:T(8,128)S(1)} %broadcast_select_fusion.21), channel_id=1, source_target_pairs={{0,1},{1,2},{2,3},{3,4},{4,5},{5,6},{6,7},{7,8},{8,9},{9,10},{10,1... | collective-permute-start | bytes 1572872 | tf_op jit(solution)/shard_map/ppermute | solution.py:17
  383.1 5.2 fusion.369
  391.8 10.3 %collective-permute-start.15 = (f32[4,64,512]{2,1,0:T(8,128)}, f32[4,64,512]{2,1,0:T(8,128)}, u32[]{:S(2)}, u32[]{:S(2)}) collective-permute-start(f32[4,64,512]{2,1,0:T(8,128)} %broadcast_select_fusion.23), channel_id=1, source_target_pairs={{0,1},{1,2},{2,3},{3,4},{4,5},{5,6},{6,7},{7,8},{8,9},{9,10},{10,1... | collective-permute-start | bytes 1572872 | tf_op jit(solution)/shard_map/ppermute | solution.py:17
  406.4 5.8 fusion.370
  423.0 8.6 collective-permute-start.17
  441.1 10.3 %collective-permute-start.19 = (f32[4,64,512]{2,1,0:T(8,128)S(1)}, f32[4,64,512]{2,1,0:T(8,128)}, u32[]{:S(2)}, u32[]{:S(2)}) collective-permute-start(f32[4,64,512]{2,1,0:T(8,128)S(1)} %bitcast_multiply_fusion.5), channel_id=1, source_target_pairs={{0,1},{1,2},{2,3},{3,4},{4,5},{5,6},{6,7},{7,8},{8,9},{9,10},{10,1... | collective-permute-start | bytes 1572872 | tf_op jit(solution)/shard_map/ppermute | solution.py:17
  456.8 4.8 fusion.103
  467.6 7.0 collective-permute-start.21
  484.7 10.4 %collective-permute-start.23 = (f32[4,64,512]{2,1,0:T(8,128)}, f32[4,64,512]{2,1,0:T(8,128)}, u32[]{:S(2)}, u32[]{:S(2)}) collective-permute-start(f32[4,64,512]{2,1,0:T(8,128)} %bitcast_multiply_fusion.3), channel_id=1, source_target_pairs={{0,1},{1,2},{2,3},{3,4},{4,5},{5,6},{6,7},{7,8},{8,9},{9,10},{10,1... | collective-permute-start | bytes 1572872 | tf_op jit(solution)/shard_map/ppermute | solution.py:17
  495.1 10.2 %gather_fusion.5 = f32[256]{0:T(256)S(1)} fusion(f32[131072]{0:T(1024)} %get-tuple-element.119, s32[1024]{0:T(1024)S(1)} %pad_clamp_fusion), kind=kCustom, calls=%fused_computation.5 | custom fusion | bytes 3072 | tf_op jit(solution)/shard_map/gather | solution.py:123
  509.2 5.7 fusion.67
  520.9 4.2 collective-permute-start.25
  539.6 12.6 %collective-permute-start.27 = (f32[4,64,512]{2,1,0:T(8,128)}, f32[4,64,512]{2,1,0:T(8,128)}, u32[]{:S(2)}, u32[]{:S(2)}) collective-permute-start(f32[4,64,512]{2,1,0:T(8,128)} %bitcast_multiply_fusion.1), channel_id=1, source_target_pairs={{0,1},{1,2},{2,3},{3,4},{4,5},{5,6},{6,7},{7,8},{8,9},{9,10},{10,1... | collective-permute-start | bytes 1572872 | tf_op jit(solution)/shard_map/ppermute | solution.py:17
  552.2 10.3 %gather_fusion.7 = f32[256]{0:T(256)S(1)} fusion(f32[131072]{0:T(1024)} %get-tuple-element.121, s32[1024]{0:T(1024)S(1)} %pad_clamp_fusion), kind=kCustom, calls=%fused_computation.7 | custom fusion | bytes 3072 | tf_op jit(solution)/shard_map/gather | solution.py:123
  562.5 10.3 %gather_fusion.8 = f32[256]{0:T(256)S(1)} fusion(f32[131072]{0:T(1024)} %get-tuple-element.122, s32[1024]{0:T(1024)S(1)} %pad_clamp_fusion), kind=kCustom, calls=%fused_computation.8 | custom fusion | bytes 3072 | tf_op jit(solution)/shard_map/gather | solution.py:123
  574.9 5.7 fusion.31
  606.1 4.3 select_add_fusion
  611.7 121.4 %all-gather.9.cloned.1.call-done = f32[64,64,512]{2,1,0:T(8,128)} async-done(((f32[4,64,512]{2,1,0:T(8,128)}), f32[64,64,512]{2,1,0:T(8,128)}) %all-gather.9.cloned.1.call-update) | async-done | bytes 8388624 | tf_op jit(solution)/shard_map/all_gather | solution.py:134
  734.2 4.5 broadcast_select_fusion
  738.6 167.0 %reduce-scatter.2.cloned.1.call-done = f32[2,4,64,512]{3,2,1,0:T(8,128)} async-done(((f32[16,4,64,512]{3,2,1,0:T(8,128)}), f32[2,4,64,512]{3,2,1,0:T(8,128)}) %reduce-scatter.2.cloned.1.call-update) | async-done | bytes 1048592 | tf_op jit(solution)/shard_map/reduce_scatter | solution.py:138
  (264 shorter events, 153.8 us)
Async XLA Ops:
  6.5 173.4 %all-gather.7.cloned.1.call-start = ((), (), s32[]{:S(2)}) async-start(), calls=%async_computation.2 | async-start | bytes 9437184 | tf_op jit(solution)/shard_map/all_gather | solution.py:89
  7.3 255.9 %all-gather.11.cloned.1.call-start = ((), (), s32[]{:S(2)}) async-start(), calls=%async_computation.4 | async-start | bytes 8912896 | tf_op jit(solution)/shard_map/all_gather | solution.py:96
  181.8 551.3 %all-gather.9.cloned.1.call-start = ((), (), s32[]{:S(2)}) async-start(), calls=%async_computation.3 | async-start | bytes 8912896 | tf_op jit(solution)/shard_map/all_gather | solution.py:134
  181.9 9.0 collective-permute-start
  183.2 7.7 collective-permute-start.1
  268.3 5.2 collective-permute-start.2
  282.7 11.4 %collective-permute-start.4 = (f32[4,64,512]{2,1,0:T(8,128)S(1)}, f32[4,64,512]{2,1,0:T(8,128)}, u32[]{:S(2)}, u32[]{:S(2)}) collective-permute-start(f32[4,64,512]{2,1,0:T(8,128)S(1)} %broadcast_select_fusion.10), channel_id=1, source_target_pairs={{1,0},{2,1},{3,2},{4,3},{5,4},{6,5},{7,6},{8,7},{9,8},{10,9},{11,1... | collective-permute-start | bytes 1572872 | tf_op jit(solution)/shard_map/ppermute | solution.py:19
  284.0 10.4 %collective-permute-start.5 = (f32[4,64,512]{2,1,0:T(8,128)S(1)}, f32[4,64,512]{2,1,0:T(8,128)}, u32[]{:S(2)}, u32[]{:S(2)}) collective-permute-start(f32[4,64,512]{2,1,0:T(8,128)S(1)} %broadcast_select_fusion.10), channel_id=1, source_target_pairs={{0,1},{1,2},{2,3},{3,4},{4,5},{5,6},{6,7},{7,8},{8,9},{9,10},{10,1... | collective-permute-start | bytes 1572872 | tf_op jit(solution)/shard_map/ppermute | solution.py:17
  303.7 12.6 %collective-permute-start.6 = (f32[4,64,512]{2,1,0:T(8,128)S(1)}, f32[4,64,512]{2,1,0:T(8,128)}, u32[]{:S(2)}, u32[]{:S(2)}) collective-permute-start(f32[4,64,512]{2,1,0:T(8,128)S(1)} %broadcast_select_fusion.12), channel_id=1, source_target_pairs={{1,0},{2,1},{3,2},{4,3},{5,4},{6,5},{7,6},{8,7},{9,8},{10,9},{11,1... | collective-permute-start | bytes 1572872 | tf_op jit(solution)/shard_map/ppermute | solution.py:19
  305.0 11.3 %collective-permute-start.7 = (f32[4,64,512]{2,1,0:T(8,128)S(1)}, f32[4,64,512]{2,1,0:T(8,128)}, u32[]{:S(2)}, u32[]{:S(2)}) collective-permute-start(f32[4,64,512]{2,1,0:T(8,128)S(1)} %broadcast_select_fusion.12), channel_id=1, source_target_pairs={{0,1},{1,2},{2,3},{3,4},{4,5},{5,6},{6,7},{7,8},{8,9},{9,10},{10,1... | collective-permute-start | bytes 1572872 | tf_op jit(solution)/shard_map/ppermute | solution.py:17
  325.8 12.0 %collective-permute-start.8 = (f32[4,64,512]{2,1,0:T(8,128)S(1)}, f32[4,64,512]{2,1,0:T(8,128)}, u32[]{:S(2)}, u32[]{:S(2)}) collective-permute-start(f32[4,64,512]{2,1,0:T(8,128)S(1)} %broadcast_select_fusion.15), channel_id=1, source_target_pairs={{1,0},{2,1},{3,2},{4,3},{5,4},{6,5},{7,6},{8,7},{9,8},{10,9},{11,1... | collective-permute-start | bytes 1572872 | tf_op jit(solution)/shard_map/ppermute | solution.py:19
  327.1 10.8 %collective-permute-start.9 = (f32[4,64,512]{2,1,0:T(8,128)S(1)}, f32[4,64,512]{2,1,0:T(8,128)}, u32[]{:S(2)}, u32[]{:S(2)}) collective-permute-start(f32[4,64,512]{2,1,0:T(8,128)S(1)} %broadcast_select_fusion.15), channel_id=1, source_target_pairs={{0,1},{1,2},{2,3},{3,4},{4,5},{5,6},{6,7},{7,8},{8,9},{9,10},{10,1... | collective-permute-start | bytes 1572872 | tf_op jit(solution)/shard_map/ppermute | solution.py:17
  347.5 12.4 %collective-permute-start.10 = (f32[4,64,512]{2,1,0:T(8,128)S(1)}, f32[4,64,512]{2,1,0:T(8,128)}, u32[]{:S(2)}, u32[]{:S(2)}) collective-permute-start(f32[4,64,512]{2,1,0:T(8,128)S(1)} %broadcast_select_fusion.18), channel_id=1, source_target_pairs={{1,0},{2,1},{3,2},{4,3},{5,4},{6,5},{7,6},{8,7},{9,8},{10,9},{11,1... | collective-permute-start | bytes 1572872 | tf_op jit(solution)/shard_map/ppermute | solution.py:19
  348.8 11.3 %collective-permute-start.11 = (f32[4,64,512]{2,1,0:T(8,128)S(1)}, f32[4,64,512]{2,1,0:T(8,128)}, u32[]{:S(2)}, u32[]{:S(2)}) collective-permute-start(f32[4,64,512]{2,1,0:T(8,128)S(1)} %broadcast_select_fusion.18), channel_id=1, source_target_pairs={{0,1},{1,2},{2,3},{3,4},{4,5},{5,6},{6,7},{7,8},{8,9},{9,10},{10,1... | collective-permute-start | bytes 1572872 | tf_op jit(solution)/shard_map/ppermute | solution.py:17
  368.5 12.7 %collective-permute-start.12 = (f32[4,64,512]{2,1,0:T(8,128)S(1)}, f32[4,64,512]{2,1,0:T(8,128)}, u32[]{:S(2)}, u32[]{:S(2)}) collective-permute-start(f32[4,64,512]{2,1,0:T(8,128)S(1)} %broadcast_select_fusion.21), channel_id=1, source_target_pairs={{1,0},{2,1},{3,2},{4,3},{5,4},{6,5},{7,6},{8,7},{9,8},{10,9},{11,1... | collective-permute-start | bytes 1572872 | tf_op jit(solution)/shard_map/ppermute | solution.py:19
  370.0 11.3 %collective-permute-start.13 = (f32[4,64,512]{2,1,0:T(8,128)S(1)}, f32[4,64,512]{2,1,0:T(8,128)}, u32[]{:S(2)}, u32[]{:S(2)}) collective-permute-start(f32[4,64,512]{2,1,0:T(8,128)S(1)} %broadcast_select_fusion.21), channel_id=1, source_target_pairs={{0,1},{1,2},{2,3},{3,4},{4,5},{5,6},{6,7},{7,8},{8,9},{9,10},{10,1... | collective-permute-start | bytes 1572872 | tf_op jit(solution)/shard_map/ppermute | solution.py:17
  390.5 13.7 %collective-permute-start.14 = (f32[4,64,512]{2,1,0:T(8,128)}, f32[4,64,512]{2,1,0:T(8,128)}, u32[]{:S(2)}, u32[]{:S(2)}) collective-permute-start(f32[4,64,512]{2,1,0:T(8,128)} %broadcast_select_fusion.23), channel_id=1, source_target_pairs={{1,0},{2,1},{3,2},{4,3},{5,4},{6,5},{7,6},{8,7},{9,8},{10,9},{11,1... | collective-permute-start | bytes 1572872 | tf_op jit(solution)/shard_map/ppermute | solution.py:19
  391.8 12.4 %collective-permute-start.15 = (f32[4,64,512]{2,1,0:T(8,128)}, f32[4,64,512]{2,1,0:T(8,128)}, u32[]{:S(2)}, u32[]{:S(2)}) collective-permute-start(f32[4,64,512]{2,1,0:T(8,128)} %broadcast_select_fusion.23), channel_id=1, source_target_pairs={{0,1},{1,2},{2,3},{3,4},{4,5},{5,6},{6,7},{7,8},{8,9},{9,10},{10,1... | collective-permute-start | bytes 1572872 | tf_op jit(solution)/shard_map/ppermute | solution.py:17
  421.5 10.1 %collective-permute-start.16 = (f32[4,64,512]{2,1,0:T(8,128)S(1)}, f32[4,64,512]{2,1,0:T(8,128)S(1)}, u32[]{:S(2)}, u32[]{:S(2)}) collective-permute-start(f32[4,64,512]{2,1,0:T(8,128)S(1)} %bitcast_multiply_fusion.6), channel_id=1, source_target_pairs={{1,0},{2,1},{3,2},{4,3},{5,4},{6,5},{7,6},{8,7},{9,8},{10,9},{11,1... | collective-permute-start | bytes 1572872 | tf_op jit(solution)/shard_map/ppermute | solution.py:19
  423.0 9.9 %collective-permute-start.17 = (f32[4,64,512]{2,1,0:T(8,128)S(1)}, f32[4,64,512]{2,1,0:T(8,128)S(1)}, u32[]{:S(2)}, u32[]{:S(2)}) collective-permute-start(f32[4,64,512]{2,1,0:T(8,128)S(1)} %bitcast_multiply_fusion.6), channel_id=1, source_target_pairs={{0,1},{1,2},{2,3},{3,4},{4,5},{5,6},{6,7},{7,8},{8,9},{9,10},{10,1... | collective-permute-start | bytes 1572872 | tf_op jit(solution)/shard_map/ppermute | solution.py:17
  439.8 15.1 %collective-permute-start.18 = (f32[4,64,512]{2,1,0:T(8,128)S(1)}, f32[4,64,512]{2,1,0:T(8,128)}, u32[]{:S(2)}, u32[]{:S(2)}) collective-permute-start(f32[4,64,512]{2,1,0:T(8,128)S(1)} %bitcast_multiply_fusion.5), channel_id=1, source_target_pairs={{1,0},{2,1},{3,2},{4,3},{5,4},{6,5},{7,6},{8,7},{9,8},{10,9},{11,1... | collective-permute-start | bytes 1572872 | tf_op jit(solution)/shard_map/ppermute | solution.py:19
  441.1 13.8 %collective-permute-start.19 = (f32[4,64,512]{2,1,0:T(8,128)S(1)}, f32[4,64,512]{2,1,0:T(8,128)}, u32[]{:S(2)}, u32[]{:S(2)}) collective-permute-start(f32[4,64,512]{2,1,0:T(8,128)S(1)} %bitcast_multiply_fusion.5), channel_id=1, source_target_pairs={{0,1},{1,2},{2,3},{3,4},{4,5},{5,6},{6,7},{7,8},{8,9},{9,10},{10,1... | collective-permute-start | bytes 1572872 | tf_op jit(solution)/shard_map/ppermute | solution.py:17
  466.2 8.4 collective-permute-start.20
  467.6 8.1 collective-permute-start.21
  483.4 23.7 %collective-permute-start.22 = (f32[4,64,512]{2,1,0:T(8,128)}, f32[4,64,512]{2,1,0:T(8,128)}, u32[]{:S(2)}, u32[]{:S(2)}) collective-permute-start(f32[4,64,512]{2,1,0:T(8,128)} %bitcast_multiply_fusion.3), channel_id=1, source_target_pairs={{1,0},{2,1},{3,2},{4,3},{5,4},{6,5},{7,6},{8,7},{9,8},{10,9},{11,1... | collective-permute-start | bytes 1572872 | tf_op jit(solution)/shard_map/ppermute | solution.py:19
  484.7 22.4 %collective-permute-start.23 = (f32[4,64,512]{2,1,0:T(8,128)}, f32[4,64,512]{2,1,0:T(8,128)}, u32[]{:S(2)}, u32[]{:S(2)}) collective-permute-start(f32[4,64,512]{2,1,0:T(8,128)} %bitcast_multiply_fusion.3), channel_id=1, source_target_pairs={{0,1},{1,2},{2,3},{3,4},{4,5},{5,6},{6,7},{7,8},{8,9},{9,10},{10,1... | collective-permute-start | bytes 1572872 | tf_op jit(solution)/shard_map/ppermute | solution.py:17
  519.5 5.7 collective-permute-start.24
  520.9 5.6 collective-permute-start.25
  538.3 34.5 %collective-permute-start.26 = (f32[4,64,512]{2,1,0:T(8,128)}, f32[4,64,512]{2,1,0:T(8,128)}, u32[]{:S(2)}, u32[]{:S(2)}) collective-permute-start(f32[4,64,512]{2,1,0:T(8,128)} %bitcast_multiply_fusion.1), channel_id=1, source_target_pairs={{1,0},{2,1},{3,2},{4,3},{5,4},{6,5},{7,6},{8,7},{9,8},{10,9},{11,1... | collective-permute-start | bytes 1572872 | tf_op jit(solution)/shard_map/ppermute | solution.py:19
  539.6 33.2 %collective-permute-start.27 = (f32[4,64,512]{2,1,0:T(8,128)}, f32[4,64,512]{2,1,0:T(8,128)}, u32[]{:S(2)}, u32[]{:S(2)}) collective-permute-start(f32[4,64,512]{2,1,0:T(8,128)} %bitcast_multiply_fusion.1), channel_id=1, source_target_pairs={{0,1},{1,2},{2,3},{3,4},{4,5},{5,6},{6,7},{7,8},{8,9},{9,10},{10,1... | collective-permute-start | bytes 1572872 | tf_op jit(solution)/shard_map/ppermute | solution.py:17
  589.7 5.2 collective-permute-start.28
  610.5 295.2 %reduce-scatter.2.cloned.1.call-start = ((), (), s32[]{:S(2)}) async-start(), calls=%async_computation.1 | async-start | bytes 9437184 | tf_op jit(solution)/shard_map/reduce_scatter | solution.py:138
  (50 other events, 1186.8 us)
Sparse Core Ops, SparseCore 0:
  9.0 170.8 all-gather.6
  182.3 80.8 all-gather.10
  610.6 122.4 all-gather.8
  738.8 166.8 reduce-scatter.1
where the time goes:
time: 927 us; the launch traced here: 915 us
  waiting for transfers between devices  533 us (57%)
  starting transfers between devices  146 us (16%)
  other arithmetic  146 us (16%)
  local copies, waits for them, and re-layouts  66 us (7%)
  between operations  24.2 us (3%)
    all_gather x1, waiting for transfers between devices, local(): piece = lax.all_gather(share, 'shot', axis=0, tiled=True)  167 us
    reduce_scatter x1, waiting for transfers between devices, local(): lax.psum_scatter(jnp.where(inside[:, None, None, None], grad_col[None], 0...  167 us
    ppermute x15, starting transfers between devices, padded_2(): lax.ppermute(tail, axis, [(i, (i + 1) % count) for i in range(ends)])  125 us
    all_gather x1, waiting for transfers between devices, local(): every_grad = lax.all_gather(grad[None], 'dom', axis=0, tiled=True)  121 us
    all_gather x1, waiting for transfers between devices, local(): everyone = lax.all_gather(local_pick[None], 'dom', axis=0, tiled=True)  70.6 us
    add x8, other arithmetic, local(): u_next = 2.0 * u_cur - u_prev + slab * lap  40.5 us
    gather x8, local copies, waits for them, and re-layouts, local(): samples.append(u_cur.reshape(-1)[rec_index])  39.4 us
    select_n x7, other arithmetic, local(): jnp.where(active, p_next, p_cur)  25.1 us
  transfers between devices with their start and end apart: 34, of which 12 were waited for; matrix products, arithmetic and copies ran while one was open for 5% of the time, Pallas kernels for 0%

commit v1 on v0

v1 whole, which is shorter than its diff:
```python
import functools

import jax
import jax.numpy as jnp
from jax import lax
from jax.experimental import pallas as pl
from jax.experimental.pallas import tpu as pltpu
from jax.sharding import PartitionSpec as P

C0, C1, C2, C3, C4 = (-205.0 / 72.0, 8.0 / 5.0, -1.0 / 5.0, 8.0 / 315.0, -1.0 / 560.0)
MESH = pl.DeviceIdType.MESH
F32 = jnp.float32
SHOTS, DOM, STEPS = 8, 16, 8
HALO = 8
PLANES, ROWS = 48, 48


def chunk_of(d):
    return d + (d // 8) * (23 - 2 * d)


class Stencil:
    def __init__(self):
        lane = lax.broadcasted_iota(jnp.int32, (8, 128), 1)
        y = lane & 63
        self.low = lane < 64
        self.up = [y >= k for k in (1, 2, 3, 4)]
        self.down = [y < 64 - k for k in (1, 2, 3, 4)]

    def __call__(self, ref, z, i):
        row = 8 + 8 * i
        mid = ref[z, pl.ds(row, 8), :]
        pairs = []
        for k in (1, 2, 3, 4):
            along_z = ref[z + k, pl.ds(row, 8), :] + ref[z - k, pl.ds(row, 8), :]
            ahead = pltpu.roll(jnp.where(self.up[k - 1], mid, 0.0), 128 - k, 1)
            behind = pltpu.roll(jnp.where(self.down[k - 1], mid, 0.0), k, 1)
            pairs.append(along_z + (ahead + behind))
        up1 = ref[z, pl.ds(row + 1, 8), :]
        up2 = ref[z, pl.ds(row + 2, 8), :]
        dn1 = ref[z, pl.ds(row - 1, 8), :]
        dn2 = ref[z, pl.ds(row - 2, 8), :]
        pairs[1] = pairs[1] + (up1 + dn1)
        pairs[3] = pairs[3] + (up2 + dn2)
        odd = C1 * (jnp.where(self.low, up1, mid) + jnp.where(self.low, mid, dn1))
        odd = odd + C3 * (jnp.where(self.low, up2, up1) + jnp.where(self.low, dn1, dn2))
        total = (3.0 * C0) * mid + C1 * pairs[0] + C2 * pairs[1] + C3 * pairs[2] + C4 * pairs[3]
        return mid, total + pltpu.roll(odd, 64, 1)


def kernel(
    vel, fwd_cur, fwd_prev, adj_cur, adj_prev, rec_pos, observed, wavelet, src_pos, count, aperture, block_slot,
    out,
    v_in, v_t, v_1, v_2, picks, m_2, f_in, f_t, f_1,
    u_a, u_b, p_c, p_p, w_a, w_b, m_x, laps, res, hits, onehot, grad, land, land_m, land_p,
    g_send, g_recv, batch, batch_1, batch_t,
    in_sem, own_sem, va_s, va_r, f_s, f_r, vb_s, vb_r, vc_s, vc_r, gd_s, gd_r, gf_s, gf_r, gg_s, gg_r,
    h_s, h_r, hm_s, hm_r, hp_s, hp_r,
):
    s, d = lax.axis_index("shot"), lax.axis_index("dom")
    e = chunk_of(d)

    v_load = pltpu.make_async_copy(vel, v_in, in_sem.at[4])
    v_load.start()
    loads = []
    for f, ref in enumerate((fwd_cur, fwd_prev, adj_cur, adj_prev)):
        loads.append(pltpu.make_async_copy(ref, f_in.at[f], in_sem.at[f]))
        loads[-1].start()

    barrier = pltpu.get_barrier_semaphore()
    for o in range(1, DOM):
        pl.semaphore_signal(barrier, inc=1, device_id=(s, lax.rem(d + o, DOM)), device_id_type=MESH)
    for o in range(1, SHOTS):
        pl.semaphore_signal(barrier, inc=1, device_id=(lax.rem(s + o, SHOTS), d), device_id_type=MESH)

    def over_dom(src, dst, send, recv):
        def copy(o):
            p = lax.rem(d + o, DOM)
            return pltpu.make_async_remote_copy(
                src_ref=src(p), dst_ref=dst, send_sem=send(o), recv_sem=recv(o), device_id=(s, p), device_id_type=MESH
            )

        return copy, DOM

    def over_shot(src, dst, send, recv):
        def copy(o):
            p = lax.rem(s + o, SHOTS)
            return pltpu.make_async_remote_copy(
                src_ref=src(p), dst_ref=dst, send_sem=send(o), recv_sem=recv(o), device_id=(p, d), device_id_type=MESH
            )

        return copy, SHOTS

    def start(exchange, own):
        copy, n = exchange

        def body(o, c):
            copy(o).start()
            return c

        lax.fori_loop(1, n, body, 0)
        own.start()

    def finish(exchange, own):
        copy, n = exchange

        def body(o, c):
            copy(o).wait()
            return c

        lax.fori_loop(1, n, body, 0)
        own.wait()

    def transpose_in(src, dst):
        def body(q, c):
            for xp in range(2):
                block = src[pl.ds(2 * xp, 2), :, pl.ds(pl.multiple_of(q * 128, 128), 128)]
                dst[xp, pl.ds(q * 128, 128), :] = block.reshape(128, 128).T
            return c

        lax.fori_loop(0, 4, body, 0)

    v_load.wait()
    for slot in range(2):
        transpose_in(v_in.at[slot], v_t.at[slot])
    pl.semaphore_wait(barrier, DOM + SHOTS - 2)

    def z_of(p):
        return pl.ds(chunk_of(p) * 32, 32)

    va = over_dom(lambda p: v_t.at[:, :, z_of(p), :], v_1.at[:, d], lambda o: va_s.at[o], lambda o: va_r.at[o])
    va_own = pltpu.make_async_copy(v_t.at[:, :, z_of(d), :], v_1.at[:, d], own_sem.at[0])
    start(va, va_own)

    fields, fields_own = [], []
    for f in range(4):
        fields.append(
            over_dom(
                lambda p, f=f: f_t.at[f, :, z_of(p), :],
                f_1.at[f, pl.ds(2 * d, 2)],
                lambda o, f=f: f_s.at[f, o],
                lambda o, f=f: f_r.at[f, o],
            )
        )
        fields_own.append(pltpu.make_async_copy(f_t.at[f, :, z_of(d), :], f_1.at[f, pl.ds(2 * d, 2)], own_sem.at[1 + f]))
    for f in range(2):
        loads[f].wait()
        transpose_in(f_in.at[f], f_t.at[f])
        start(fields[f], fields_own[f])
    for f in range(2, 4):
        loads[f].wait()
        transpose_in(f_in.at[f], f_t.at[f])

    pos = rec_pos[...]
    rec_row = (((pos & 511) - 32 * e + 4) << 5) + (pos >> 16)
    rec_lane = (((pos >> 15) & 1) << 6) + ((pos >> 9) & 63)
    row_id = lax.broadcasted_iota(jnp.int32, (256, 256), 0)
    for g in range(5):
        onehot[g] = (row_id + 256 * g == rec_row).astype(F32).astype(jnp.bfloat16)
    lanes = (lax.broadcasted_iota(jnp.int32, (128, 256), 0) == rec_lane).astype(F32)

    def dot(g, b):
        found = lax.dot_general(onehot[g], b, (((1,), (1,)), ((), ())), preferred_element_type=F32)
        return found.reshape(8, 32, 128)

    ones = lanes.astype(jnp.bfloat16)
    for g in range(5):
        hits[pl.ds(8 * g, 8)] = dot(g, ones)

    def record(t, c):
        b = lanes * observed[pl.ds(t, 1), :]
        high = b.astype(jnp.bfloat16)
        low = (b - high.astype(F32)).astype(jnp.bfloat16)
        for g in range(5):
            res[t, pl.ds(8 * g, 8)] = dot(g, high) + dot(g, low)
        return c

    lax.fori_loop(0, STEPS, record, 0)

    def clear(z, c):
        for ref in (u_a, u_b, p_c, p_p, w_a, w_b, m_x):
            ref[z] = jnp.zeros((ROWS, 128), F32)
        return c

    lax.fori_loop(0, PLANES, clear, 0)

    finish(va, va_own)
    vb = over_shot(
        lambda p: v_1.at[:, :, p // 4, pl.ds(lax.rem(p, 4) * 8, 8), :],
        v_2.at[pl.ds(2 * s, 2)],
        lambda o: vb_s.at[o],
        lambda o: vb_r.at[o],
    )
    vb_own = pltpu.make_async_copy(
        v_1.at[:, :, s // 4, pl.ds(lax.rem(s, 4) * 8, 8), :], v_2.at[pl.ds(2 * s, 2)], own_sem.at[5]
    )
    start(vb, vb_own)

    def relayout(f, dst):
        flat = dst.reshape(PLANES * ROWS, 128)

        def body(r, c):
            for g in range(4):
                flat[pl.ds((HALO + 8 * g) * ROWS + 8 + r, 8, stride=ROWS), :] = f_1[f, r, pl.ds(8 * g, 8), :]
            return c

        lax.fori_loop(0, 32, body, 0)

    def halo(src, n, land_ref, send, recv):
        def ends():
            right = pltpu.make_async_remote_copy(
                src_ref=src.at[pl.ds(HALO + 32 - n, n), pl.ds(8, 32), :],
                dst_ref=land_ref.at[0],
                send_sem=send.at[0],
                recv_sem=recv.at[0],
                device_id=(s, chunk_of(lax.rem(e + 1, DOM))),
                device_id_type=MESH,
            )
            left = pltpu.make_async_remote_copy(
                src_ref=src.at[pl.ds(HALO, n), pl.ds(8, 32), :],
                dst_ref=land_ref.at[1],
                send_sem=send.at[1],
                recv_sem=recv.at[1],
                device_id=(s, chunk_of(lax.rem(e + DOM - 1, DOM))),
                device_id_type=MESH,
            )
            return right, left

        def begin():
            right, left = ends()
            pl.when(e < DOM - 1)(right.start)
            pl.when(e > 0)(left.start)

        def sent():
            right, left = ends()
            pl.when(e < DOM - 1)(right.wait_send)
            pl.when(e > 0)(left.wait_send)

        def arrived(use):
            right, left = ends()

            @pl.when(e > 0)
            def _():
                right.wait_recv()
                use(0, HALO - n)

            @pl.when(e < DOM - 1)
            def _():
                left.wait_recv()
                use(1, HALO + 32)

        return begin, sent, arrived

    def put(dst, land_ref, n):
        def use(side, at):
            def body(z, c):
                dst[at + z, pl.ds(8, 32), :] = land_ref[side, z]
                return c

            lax.fori_loop(0, n, body, 0)

        return use

    for f, dst in ((0, u_a), (1, u_b)):
        finish(fields[f], fields_own[f])
        relayout(f, dst)
    begin, sent, arrived = halo(u_b, 4, land_p.at[0], hp_s.at[0], hp_r.at[0])
    begin()

    finish(vb, vb_own)

    def pick(q, c):
        shot, k = q // 16, lax.rem(q, 16)
        block = aperture[shot, k]
        block_x = block >> 3
        slot = block_slot[((block_x >> 4) << 3) + (block & 7)]
        picks[shot, k] = v_2[slot, block_x & 15]
        return c

    lax.fori_loop(0, SHOTS * 16, pick, 0)
    vc = over_shot(lambda p: picks.at[p], m_2.at[s], lambda o: vc_s.at[o], lambda o: vc_r.at[o])
    vc_own = pltpu.make_async_copy(picks.at[s], m_2.at[s], own_sem.at[6])
    start(vc, vc_own)
    arrived(put(u_b, land_p.at[0], 4))
    sent()
    finish(vc, vc_own)
    m_flat = m_x.reshape(PLANES * ROWS, 128)

    def place(k, c):
        for xp in range(2):
            for g in range(4):
                m_flat[pl.ds((HALO + 8 * g) * ROWS + 8 + xp + 2 * k, 8, stride=ROWS), :] = m_2[4 * xp + g, k]
        return c

    lax.fori_loop(0, 16, place, 0)
    begin, sent, arrived = halo(m_x, 8, land_m, hm_s, hm_r)
    begin()
    arrived(put(m_x, land_m, 8))
    sent()
    for f in range(2, 4):
        start(fields[f], fields_own[f])

    lap_of = Stencil()
    source = src_pos[0]
    src_z = (source & 511) - 32 * e + HALO
    src_cell = ((source >> 16) << 7) + (((source >> 15) & 1) << 6) + ((source >> 9) & 63)
    cell = (lax.broadcasted_iota(jnp.int32, (8, 128), 0) << 7) + lax.broadcasted_iota(jnp.int32, (8, 128), 1)
    steps = jnp.full((8, 128), count[0], jnp.int32)

    def tile(i):
        return pl.ds(8 + 8 * i, 8)

    def forward(src, dst, lo, hi, t):
        active = steps > t

        def body(z, c):
            amount = jnp.where(z == src_z, wavelet[t], 0.0)
            for i in range(4):
                mid, lap = lap_of(src, z, i)
                inner = pl.ds(8 * i, 8)
                laps[t, z - 4, inner, :] = lap
                u = 2.0 * mid - dst[z, tile(i), :] + m_x[z, tile(i), :] * lap
                u = u + jnp.where(cell + 1024 * i == src_cell, amount, 0.0)
                dst[z, tile(i), :] = u
                res[t, z - 4, inner, :] = jnp.where(
                    active, hits[z - 4, inner, :] * u - res[t, z - 4, inner, :], 0.0
                )
            return c

        lax.fori_loop(lo, hi, body, 0)

    def fwd_pair(i, c):
        par = lax.rem(i, 2)
        begin, sent, arrived = halo(u_a, 8, land.at[par], h_s.at[par], h_r.at[par])
        begin()
        arrived(put(u_a, land.at[par], 8))
        forward(u_a, u_b, 4, 44, 2 * i)
        sent()
        forward(u_b, u_a, 8, 40, 2 * i + 1)
        return c

    lax.fori_loop(0, STEPS // 2, fwd_pair, 0)

    for f, dst in ((2, p_c), (3, p_p)):
        finish(fields[f], fields_own[f])
        relayout(f, dst)
    begin, sent, arrived = halo(p_p, 4, land_p.at[1], hp_s.at[1], hp_r.at[1])
    begin()

    active = steps > STEPS - 1

    def first(z, c):
        for i in range(4):
            inner = pl.ds(8 * i, 8)
            hit = p_c[z, tile(i), :] + res[STEPS - 1, z - 4, inner, :]
            p_c[z, tile(i), :] = hit
            w_a[z, tile(i), :] = m_x[z, tile(i), :] * hit
            grad[z - 4, inner, :] = jnp.where(active, hit * laps[STEPS - 1, z - 4, inner, :], 0.0)
        return c

    lax.fori_loop(8, 40, first, 0)

    def clear_ends(z, c):
        grad[z] = jnp.zeros((32, 128), F32)
        grad[36 + z] = jnp.zeros((32, 128), F32)
        return c

    lax.fori_loop(0, 4, clear_ends, 0)
    arrived(put(p_p, land_p.at[1], 4))
    sent()

    def backward(src, dst, lo, hi, t):
        active = steps > t
        then = steps > t - 1

        def body(z, c):
            for i in range(4):
                inner = pl.ds(8 * i, 8)
                _, lap = lap_of(src, z, i)
                hit = p_c[z, tile(i), :]
                prev = p_p[z, tile(i), :]
                cur = jnp.where(active, 2.0 * hit - prev + lap, hit)
                p_p[z, tile(i), :] = jnp.where(active, hit, prev)
                hit = cur + res[t - 1, z - 4, inner, :]
                p_c[z, tile(i), :] = hit
                dst[z, tile(i), :] = m_x[z, tile(i), :] * hit
                grad[z - 4, inner, :] = grad[z - 4, inner, :] + jnp.where(
                    then, hit * laps[t - 1, z - 4, inner, :], 0.0
                )
            return c

        lax.fori_loop(lo, hi, body, 0)

    def adj_ends(land_ref, t):
        stepped = steps > t + 1

        def use(side, at):
            def keep(z, c):
                for i in range(4):
                    p_p[z, tile(i), :] = jnp.where(stepped, p_c[z, tile(i), :], p_p[z, tile(i), :])
                return c

            near = at + 4 * (1 - side)
            lax.fori_loop(near, near + 4, keep, 0)

            def body(z, c):
                hit = land_ref[side, z]
                p_c[at + z, pl.ds(8, 32), :] = hit
                w_a[at + z, pl.ds(8, 32), :] = m_x[at + z, pl.ds(8, 32), :] * hit
                return c

            lax.fori_loop(0, 8, body, 0)

        return use

    def adj_pair(i, c):
        par = lax.rem(i, 2)
        t = STEPS - 1 - 2 * i
        begin, sent, arrived = halo(p_c, 8, land.at[par], h_s.at[par], h_r.at[par])
        begin()
        arrived(adj_ends(land.at[par], t))
        sent()
        backward(w_a, w_b, 4, 44, t)

        @pl.when(i < STEPS // 2 - 1)
        def _():
            backward(w_b, w_a, 8, 40, t - 1)

        return c

    lax.fori_loop(0, STEPS // 2, adj_pair, 0)

    g_flat = grad.reshape(40 * 32, 128)

    def gather(k, c):
        for xp in range(2):
            for g in range(4):
                g_send[4 * xp + g, k] = g_flat[pl.ds((4 + 8 * g) * 32 + xp + 2 * k, 8, stride=32), :]
        return c

    lax.fori_loop(0, 16, gather, 0)
    gd = over_shot(lambda p: g_send.at[p], g_recv.at[s], lambda o: gd_s.at[o], lambda o: gd_r.at[o])
    gd_own = pltpu.make_async_copy(g_send.at[s], g_recv.at[s], own_sem.at[7])
    start(gd, gd_own)
    finish(gd, gd_own)

    def add_up(col, c):
        sums = [jnp.zeros((8, 128), F32) for _ in range(16)]
        for shot in range(SHOTS):
            base = aperture[shot, 0]
            k = (col - (base >> 3)) & 15
            block_x = (base >> 3) + k
            slot = block_slot[((block_x >> 4) << 3) + (base & 7)]
            value = g_recv[shot, k]
            slots = jnp.full((8, 128), slot, jnp.int32)
            for j in range(16):
                sums[j] = sums[j] + jnp.where(slots == j, value, 0.0)
        for j in range(16):
            batch[j, col] = sums[j]
        return c

    lax.fori_loop(0, 16, add_up, 0)
    gf = over_shot(
        lambda p: batch.at[pl.ds(2 * p, 2)],
        batch_1.at[:, :, s // 4, pl.ds(lax.rem(s, 4) * 8, 8), :],
        lambda o: gf_s.at[o],
        lambda o: gf_r.at[o],
    )
    gf_own = pltpu.make_async_copy(
        batch.at[pl.ds(2 * s, 2)], batch_1.at[:, :, s // 4, pl.ds(lax.rem(s, 4) * 8, 8), :], own_sem.at[8]
    )
    start(gf, gf_own)
    finish(gf, gf_own)
    gg = over_dom(lambda p: batch_1.at[:, p], batch_t.at[:, :, z_of(d), :], lambda o: gg_s.at[o], lambda o: gg_r.at[o])
    gg_own = pltpu.make_async_copy(batch_1.at[:, d], batch_t.at[:, :, z_of(d), :], own_sem.at[9])
    start(gg, gg_own)
    finish(gg, gg_own)

    def back(q, c):
        cols = pl.ds(pl.multiple_of(q * 128, 128), 128)
        for slot in range(2):
            for xp in range(2):
                v_in[slot, pl.ds(2 * xp, 2), :, cols] = batch_t[slot, xp, pl.ds(q * 128, 128), :].T.reshape(2, 64, 128)
        return c

    lax.fori_loop(0, 4, back, 0)
    store = pltpu.make_async_copy(v_in, out, in_sem.at[4])
    store.start()
    store.wait()


def local(
    velocity,
    fwd_prev,
    fwd_cur,
    adj_prev,
    adj_cur,
    wavelet,
    src_pos,
    rec_pos,
    observed,
    step_count,
    aperture,
    block_slot,
    prev_batch,
    snapshot,
):
    shape = (2, 4, 64, 512)
    hbm = pl.BlockSpec(memory_space=pl.ANY)
    vmem = pl.BlockSpec(memory_space=pltpu.VMEM)
    smem = pl.BlockSpec(memory_space=pltpu.SMEM)
    field = pltpu.VMEM((PLANES, ROWS, 128), F32)
    dma = pltpu.SemaphoreType.DMA
    scratch = [
        pltpu.VMEM(shape, F32),
        pltpu.VMEM((2, 2, 512, 128), F32),
        pltpu.VMEM((2, 16, 2, 32, 128), F32),
        pltpu.VMEM((16, 16, 8, 128), F32),
        pltpu.VMEM((8, 16, 8, 128), F32),
        pltpu.VMEM((8, 16, 8, 128), F32),
        pltpu.VMEM((4, 4, 64, 512), F32),
        pltpu.VMEM((4, 2, 512, 128), F32),
        pltpu.VMEM((4, 32, 32, 128), F32),
        *[field] * 7,
        pltpu.VMEM((STEPS, 40, 32, 128), F32),
        pltpu.VMEM((STEPS, 40, 32, 128), F32),
        pltpu.VMEM((40, 32, 128), F32),
        pltpu.VMEM((5, 256, 256), jnp.bfloat16),
        pltpu.VMEM((40, 32, 128), F32),
        pltpu.VMEM((2, 2, 8, 32, 128), F32),
        pltpu.VMEM((2, 8, 32, 128), F32),
        pltpu.VMEM((2, 2, 4, 32, 128), F32),
        pltpu.VMEM((8, 16, 8, 128), F32),
        pltpu.VMEM((8, 16, 8, 128), F32),
        pltpu.VMEM((16, 16, 8, 128), F32),
        pltpu.VMEM((2, 16, 2, 32, 128), F32),
        pltpu.VMEM((2, 2, 512, 128), F32),
        dma((5,)),
        dma((10,)),
        dma((16,)), dma((16,)),
        dma((4, 16)), dma((4, 16)),
        dma((8,)), dma((8,)),
        dma((8,)), dma((8,)),
        dma((8,)), dma((8,)),
        dma((8,)), dma((8,)),
        dma((16,)), dma((16,)),
        dma((2, 2)), dma((2, 2)),
        dma((2,)), dma((2,)),
        dma((2, 2)), dma((2, 2)),
    ]
    batch = pl.pallas_call(
        kernel,
        out_shape=jax.ShapeDtypeStruct(shape, F32),
        in_specs=[hbm] * 5 + [vmem] * 2 + [smem] * 5,
        out_specs=hbm,
        scratch_shapes=scratch,
        name="adjoint_gradient",
        compiler_params=pltpu.CompilerParams(collective_id=0, has_side_effects=True, vmem_limit_bytes=56 << 20),
    )(
        velocity.reshape(shape),
        fwd_cur[0],
        fwd_prev[0],
        adj_cur[0],
        adj_prev[0],
        rec_pos,
        observed[0],
        wavelet[0],
        src_pos,
        step_count,
        aperture,
        block_slot,
    )
    result = (batch - prev_batch.reshape(shape)) + snapshot.reshape(shape)
    return result.reshape(velocity.shape)


def solution(mesh):
    placed = (
        P("shot", "dom", None, None, None),
        P("shot", "dom", None, None),
        P("shot", "dom", None, None),
        P("shot", "dom", None, None),
        P("shot", "dom", None, None),
        P("shot", None),
        P("shot"),
        P("shot", None),
        P("shot", None, None),
        P("shot"),
        P(),
        P(),
        P("shot", "dom", None, None, None),
        P("shot", "dom", None, None, None),
    )
    return jax.shard_map(
        local,
        mesh=mesh,
        in_specs=placed,
        out_specs=P("shot", "dom", None, None, None),
        check_vma=False,
    )
```

time: 927 us -> 213 us (0.23)
  waiting for transfers between devices: 533 us -> 0 us
  Pallas kernels: 0 us -> 206 us
  starting transfers between devices: 146 us -> 0 us
  other arithmetic: 146 us -> 2.54 us
  local copies, waits for them, and re-layouts: 66 us -> 0.01 us
  between operations: 24.2 us -> 1.34 us
    all_gather x3 -> x0, waiting for transfers between devices: 359 us -> none  [the longest x1 167 us: local(): piece = lax.all_gather(share, 'shot', axis=0, tiled=True)]
    pallas_call x0 -> x1, Pallas kernels: none -> 206 us  [local(): pl.pallas_call(kernel, out_shape=jax.ShapeDtypeStruct(shape, F32), in_spe...]
    reduce_scatter x1 -> x0, waiting for transfers between devices: 167 us -> none  [local(): lax.psum_scatter(jnp.where(inside[:, None, None, None], grad_col[None], 0...]
    ppermute x30 -> x0, starting transfers between devices: 146 us -> none  [the longest x15 125 us: padded_2(): lax.ppermute(tail, axis, [(i, (i + 1) % count) for i in range(ends)])]
    add x9 -> x0, other arithmetic: 44.8 us -> none  [the longest x8 40.5 us: local(): u_next = 2.0 * u_cur - u_prev + slab * lap]
    gather x10 -> x0, local copies, waits for them, and re-layouts: 41.4 us -> none  [the longest x8 39.4 us: local(): samples.append(u_cur.reshape(-1)[rec_index])]
    select_n x24 -> x0, other arithmetic: 39 us -> none  [the longest x7 25.1 us: local(): jnp.where(active, p_next, p_cur)]
    scatter-add x16 -> x0, other arithmetic: 26.1 us -> none  [the longest x8 24.6 us: local(): p_hit = p_cur.reshape(-1).at[rec_index].add(residual).reshape(cells)]
  transfers between devices with their start and end apart: 34 -> 0, of which waited for: 12 -> 0; matrix products, arithmetic and copies ran while one was open for 5% -> 0% of each run, Pallas kernels for 0% -> 0%
where the time goes in v1:
time: 213 us; the launch traced here: 210 us
  Pallas kernels  206 us (97%)
  other arithmetic  2.54 us (1%)
    pallas_call x1, Pallas kernels, local(): pl.pallas_call(kernel, out_shape=jax.ShapeDtypeStruct(shape, F32), in_spe...  206 us

profile of v1, /device:TPU:0, one launch (start us, length us, event | category | flops | bytes accessed | tf_op | source)
XLA Modules:
  0.0 210.1 jit_solution(2952237203197709779)
XLA Ops:
  1.3 0.0 copy-start
  1.3 0.0 copy-start.1
  1.3 206.2 %adjoint_gradient.1 = f32[2,4,64,512]{3,2,1,0:T(8,128)} custom-call(f32[2,4,64,512]{3,2,1,0:T(8,128)} %bitcast.19, f32[4,64,512]{2,1,0:T(8,128)} %bitcast.20, f32[4,64,512]{2,1,0:T(8,128)} %bitcast.21, f32[4,64,512]{2,1,0:T(8,128)} %bitcast.22, f32[4,64,512]{2,1,0:T(8,128)} %bitcast.23, s32[1,256]{1,0:T(1,128)} %rec_pos.1, f32[8,256]{1,0:T(8,128)} %bitcast.24, ...), custom_call_target="tpu_custom_call" | custom-call | tf_op jit(solution)/shard_map/adjoint_gradient/pallas_call | solution.py:551
  207.5 0.0 copy-done
  207.5 0.0 copy-done.1
  207.6 2.5 %fusion = f32[2,1,4,64,512]{4,3,2,1,0:T(8,128)} fusion(f32[2,1,4,64,512]{4,3,2,1,0:T(8,128)S(1)} %copy-done, f32[2,4,64,512]{3,2,1,0:T(8,128)} %adjoint_gradient.1, f32[2,1,4,64,512]{4,3,2,1,0:T(8,128)S(1)} %copy-done.1), kind=kLoop, calls=%fused_computation.1 | loop fusion | flops 524288 | bytes 4194304 | tf_op jit(solution)/shard_map/reshape | solution.py:574
Async XLA Ops:
  1.3 206.2 %copy-start = (f32[2,1,4,64,512]{4,3,2,1,0:T(8,128)S(1)}, f32[2,1,4,64,512]{4,3,2,1,0:T(8,128)}, u32[]{:S(2)}) copy-start(f32[2,1,4,64,512]{4,3,2,1,0:T(8,128)} %param.27) | copy-start | bytes 3145732
  1.3 206.2 %copy-start.1 = (f32[2,1,4,64,512]{4,3,2,1,0:T(8,128)S(1)}, f32[2,1,4,64,512]{4,3,2,1,0:T(8,128)}, u32[]{:S(2)}) copy-start(f32[2,1,4,64,512]{4,3,2,1,0:T(8,128)} %param.26) | copy-start | bytes 3145732

commit v2 on v1

v2 whole, which is shorter than its diff:
```python
import functools

import jax
import jax.numpy as jnp
from jax import lax
from jax.experimental import pallas as pl
from jax.experimental.pallas import tpu as pltpu
from jax.sharding import PartitionSpec as P

C0, C1, C2, C3, C4 = (-205.0 / 72.0, 8.0 / 5.0, -1.0 / 5.0, 8.0 / 315.0, -1.0 / 560.0)
MESH = pl.DeviceIdType.MESH
F32 = jnp.float32
SHOTS, DOM, STEPS = 8, 16, 8
HALO = 8
PLANES, ROWS = 48, 48


def chunk_of(d):
    return d + (d // 8) * (23 - 2 * d)


def band():
    row = lax.broadcasted_iota(jnp.int32, (256, 256), 0)
    col = lax.broadcasted_iota(jnp.int32, (256, 256), 1)
    gap = jnp.abs((row & 127) - (col & 127))
    same = ((row >> 6) & 1) == ((col >> 6) & 1)
    full = jnp.zeros((256, 256), F32)
    for k, c in ((1, C1), (2, C2), (3, C3), (4, C4)):
        full = full + jnp.where(same & (gap == k), c, 0.0)
    high = full.astype(jnp.bfloat16).astype(F32)
    low = jnp.where(row < 128, full - high, 0.0)
    return jnp.where(col < 128, high, low).astype(jnp.bfloat16)


def stencil(ref, z0, weights):
    low = lax.broadcasted_iota(jnp.int32, (8, 128), 1) < 64
    cells = jnp.concatenate([ref[z0 + p, pl.ds(8, 32), :] for p in range(8)], 0)
    high = cells.astype(jnp.bfloat16)
    rest = (cells - high.astype(F32)).astype(jnp.bfloat16)
    along_y = jnp.dot(jnp.concatenate([high, rest], 1), weights, preferred_element_type=F32)
    along_y = along_y[:, :128] + along_y[:, 128:]
    for p in range(8):
        z = z0 + p
        for i in range(4):
            row = 8 + 8 * i
            mid = ref[z, pl.ds(row, 8), :]
            pairs = [ref[z + k, pl.ds(row, 8), :] + ref[z - k, pl.ds(row, 8), :] for k in (1, 2, 3, 4)]
            up1, up2, dn1, dn2 = (ref[z, pl.ds(row + k, 8), :] for k in (1, 2, -1, -2))
            pairs[1] = pairs[1] + (up1 + dn1)
            pairs[3] = pairs[3] + (up2 + dn2)
            odd = C1 * (jnp.where(low, up1, mid) + jnp.where(low, mid, dn1))
            odd = odd + C3 * (jnp.where(low, up2, up1) + jnp.where(low, dn1, dn2))
            total = (3.0 * C0) * mid + C1 * pairs[0] + C2 * pairs[1] + C3 * pairs[2] + C4 * pairs[3]
            lap = total + pltpu.roll(odd, 64, 1) + along_y[32 * p + 8 * i : 32 * p + 8 * i + 8]
            yield z, i, mid, lap


def kernel(
    vel, fwd_cur, fwd_prev, adj_cur, adj_prev, rec_pos, observed, wavelet, src_pos, count, aperture, block_slot,
    out,
    v_2, picks, m_b, m_t, m_1, f_in, f_t, f_1,
    u_a, u_b, p_a, p_b, p_p, w_a, w_b, m_x, laps, res, hits, onehot, weights, grad, land, land_m, land_p,
    g_1, g_send, g_t, g_b, g_recv, batch,
    in_sem, own_sem, va_s, va_r, f_s, f_r, vb_s, vb_r, vc_s, vc_r, gd_s, gd_r, gf_s, gf_r, gg_s, gg_r,
    h_s, h_r, hm_s, hm_r, hp_s, hp_r,
):
    s, d = lax.axis_index("shot"), lax.axis_index("dom")
    e = chunk_of(d)

    loads = []
    for f, ref in enumerate((fwd_cur, fwd_prev, adj_cur, adj_prev)):
        loads.append(pltpu.make_async_copy(ref, f_in.at[f], in_sem.at[f]))
        loads[-1].start()

    barrier = pltpu.get_barrier_semaphore()
    for o in range(1, DOM):
        pl.semaphore_signal(barrier, inc=1, device_id=(s, lax.rem(d + o, DOM)), device_id_type=MESH)
    for o in range(1, SHOTS):
        pl.semaphore_signal(barrier, inc=1, device_id=(lax.rem(s + o, SHOTS), d), device_id_type=MESH)

    def over_dom(src, dst, send, recv):
        def copy(o):
            p = lax.rem(d + o, DOM)
            return pltpu.make_async_remote_copy(
                src_ref=src(p), dst_ref=dst, send_sem=send(o), recv_sem=recv(o), device_id=(s, p), device_id_type=MESH
            )

        return copy, DOM

    def over_shot(src, dst, send, recv):
        def copy(o):
            p = lax.rem(s + o, SHOTS)
            return pltpu.make_async_remote_copy(
                src_ref=src(p), dst_ref=dst, send_sem=send(o), recv_sem=recv(o), device_id=(p, d), device_id_type=MESH
            )

        return copy, SHOTS

    def start(exchange, own):
        copy, n = exchange

        def body(o, c):
            copy(o).start()
            return c

        lax.fori_loop(1, n, body, 0)
        own.start()

    def finish(exchange, own):
        copy, n = exchange

        def body(o, c):
            copy(o).wait()
            return c

        lax.fori_loop(1, n, body, 0)
        own.wait()

    def transpose_in(src, dst):
        def body(q, c):
            for xp in range(2):
                block = src[pl.ds(2 * xp, 2), :, pl.ds(pl.multiple_of(q * 128, 128), 128)]
                dst[xp, pl.ds(q * 128, 128), :] = block.reshape(128, 128).T
            return c

        lax.fori_loop(0, 4, body, 0)

    def z_of(p):
        return pl.ds(chunk_of(p) * 32, 32)

    def rows_of(p):
        return pl.ds(p * 8, 8)

    loads[0].wait()
    transpose_in(f_in.at[0], f_t.at[0])
    pl.semaphore_wait(barrier, DOM + SHOTS - 2)
    va = over_shot(
        lambda p: vel.at[:, :, rows_of(p), :], v_2.at[pl.ds(2 * s, 2)], lambda o: va_s.at[o], lambda o: va_r.at[o]
    )
    va_own = pltpu.make_async_copy(vel.at[:, :, rows_of(s), :], v_2.at[pl.ds(2 * s, 2)], own_sem.at[0])
    start(va, va_own)

    fields, fields_own = [], []
    for f in range(4):
        fields.append(
            over_dom(
                lambda p, f=f: f_t.at[f, :, z_of(p), :],
                f_1.at[f, pl.ds(2 * d, 2)],
                lambda o, f=f: f_s.at[f, o],
                lambda o, f=f: f_r.at[f, o],
            )
        )
        fields_own.append(pltpu.make_async_copy(f_t.at[f, :, z_of(d), :], f_1.at[f, pl.ds(2 * d, 2)], own_sem.at[1 + f]))
    start(fields[0], fields_own[0])
    loads[1].wait()
    transpose_in(f_in.at[1], f_t.at[1])
    start(fields[1], fields_own[1])
    for f in range(2, 4):
        loads[f].wait()
        transpose_in(f_in.at[f], f_t.at[f])

    pos = rec_pos[...]
    rec_row = (((pos & 511) - 32 * e + 4) << 5) + (pos >> 16)
    rec_lane = (((pos >> 15) & 1) << 6) + ((pos >> 9) & 63)
    row_id = lax.broadcasted_iota(jnp.int32, (256, 256), 0)
    for g in range(5):
        onehot[g] = (row_id + 256 * g == rec_row).astype(F32).astype(jnp.bfloat16)
    lanes = (lax.broadcasted_iota(jnp.int32, (128, 256), 0) == rec_lane).astype(F32)

    def dot(g, b):
        found = lax.dot_general(onehot[g], b, (((1,), (1,)), ((), ())), preferred_element_type=F32)
        return found.reshape(8, 32, 128)

    ones = lanes.astype(jnp.bfloat16)
    for g in range(5):
        hits[pl.ds(8 * g, 8)] = dot(g, ones)

    def record(t, c):
        b = lanes * observed[pl.ds(t, 1), :]
        high = b.astype(jnp.bfloat16)
        low = (b - high.astype(F32)).astype(jnp.bfloat16)
        for g in range(5):
            res[t, pl.ds(8 * g, 8)] = dot(g, high) + dot(g, low)
        return c

    lax.fori_loop(0, STEPS, record, 0)

    def clear(z, c):
        for ref in (u_a, u_b, p_a, p_b, p_p, w_a, w_b, m_x):
            ref[z] = jnp.zeros((ROWS, 128), F32)
        return c

    lax.fori_loop(0, PLANES, clear, 0)
    weights[...] = band()

    finish(va, va_own)

    def slot_of(shot, col):
        first = aperture[shot, 0]
        block_x = (first >> 3) + ((col - (first >> 3)) & 15)
        return block_slot[((block_x >> 4) << 3) + (first & 7)]

    def pick(shot, c):
        picks[shot] = v_2[slot_of(shot, d)]
        return c

    lax.fori_loop(0, SHOTS, pick, 0)
    vb = over_shot(lambda p: picks.at[p], m_b.at[:, rows_of(s), :], lambda o: vb_s.at[o], lambda o: vb_r.at[o])
    vb_own = pltpu.make_async_copy(picks.at[s], m_b.at[:, rows_of(s), :], own_sem.at[5])
    start(vb, vb_own)

    def relayout(f, dst):
        flat = dst.reshape(PLANES * ROWS, 128)

        def body(r, c):
            for g in range(4):
                flat[pl.ds((HALO + 8 * g) * ROWS + 8 + r, 8, stride=ROWS), :] = f_1[f, r, pl.ds(8 * g, 8), :]
            return c

        lax.fori_loop(0, 32, body, 0)

    def halo(src, n, land_ref, send, recv):
        def ends():
            right = pltpu.make_async_remote_copy(
                src_ref=src.at[pl.ds(HALO + 32 - n, n), pl.ds(8, 32), :],
                dst_ref=land_ref.at[0],
                send_sem=send.at[0],
                recv_sem=recv.at[0],
                device_id=(s, chunk_of(lax.rem(e + 1, DOM))),
                device_id_type=MESH,
            )
            left = pltpu.make_async_remote_copy(
                src_ref=src.at[pl.ds(HALO, n), pl.ds(8, 32), :],
                dst_ref=land_ref.at[1],
                send_sem=send.at[1],
                recv_sem=recv.at[1],
                device_id=(s, chunk_of(lax.rem(e + DOM - 1, DOM))),
                device_id_type=MESH,
            )
            return right, left

        def begin():
            right, left = ends()
            pl.when(e < DOM - 1)(right.start)
            pl.when(e > 0)(left.start)

        def sent():
            right, left = ends()
            pl.when(e < DOM - 1)(right.wait_send)
            pl.when(e > 0)(left.wait_send)

        def arrived(use):
            right, left = ends()

            @pl.when(e > 0)
            def _():
                right.wait_recv()
                use(0, HALO - n)

            @pl.when(e < DOM - 1)
            def _():
                left.wait_recv()
                use(1, HALO + 32)

        return begin, sent, arrived

    def put(dst, land_ref, n):
        def use(side, at):
            def body(z, c):
                dst[at + z, pl.ds(8, 32), :] = land_ref[side, z]
                return c

            lax.fori_loop(0, n, body, 0)

        return use

    def u_halo(par):
        return halo(u_a, 8, land.at[par], h_s.at[par], h_r.at[par])

    finish(fields[0], fields_own[0])
    relayout(0, u_a)
    u_halo(0)[0]()
    finish(fields[1], fields_own[1])
    relayout(1, u_b)
    prev_halo = halo(u_b, 4, land_p.at[0], hp_s.at[0], hp_r.at[0])
    prev_halo[0]()

    finish(vb, vb_own)
    transpose_in(m_b, m_t)
    vc = over_dom(lambda p: m_t.at[:, z_of(p), :], m_1.at[d], lambda o: vc_s.at[o], lambda o: vc_r.at[o])
    vc_own = pltpu.make_async_copy(m_t.at[:, z_of(d), :], m_1.at[d], own_sem.at[6])
    start(vc, vc_own)
    prev_halo[2](put(u_b, land_p.at[0], 4))
    prev_halo[1]()
    finish(vc, vc_own)
    for f in range(2, 4):
        start(fields[f], fields_own[f])
    m_flat = m_x.reshape(PLANES * ROWS, 128)
    base_x = aperture[s, 0] >> 3

    def place(k, c):
        slab = m_1[(base_x + k) & 15]
        for xp in range(2):
            for g in range(4):
                m_flat[pl.ds((HALO + 8 * g) * ROWS + 8 + xp + 2 * k, 8, stride=ROWS), :] = slab[xp, 8 * g : 8 * g + 8]
        return c

    lax.fori_loop(0, 16, place, 0)
    model_halo = halo(m_x, 8, land_m, hm_s, hm_r)
    model_halo[0]()

    source = src_pos[0]
    src_z = (source & 511) - 32 * e + HALO
    src_cell = ((source >> 16) << 7) + (((source >> 15) & 1) << 6) + ((source >> 9) & 63)
    cell = (lax.broadcasted_iota(jnp.int32, (8, 128), 0) << 7) + lax.broadcasted_iota(jnp.int32, (8, 128), 1)
    steps = jnp.full((8, 128), count[0], jnp.int32)

    def tile(i):
        return pl.ds(8 + 8 * i, 8)

    def inner(i):
        return pl.ds(8 * i, 8)

    def blocks(body, first, stride, n):
        def one(j, c):
            body(first + stride * j)
            return c

        lax.fori_loop(0, n, one, 0)

    def forward(src, dst, t):
        def body(z0):
            active = steps > t
            found = []
            for z, i, mid, lap in stencil(src, z0, weights[...]):
                amount = jnp.where(z == src_z, wavelet[t], 0.0)
                u = 2.0 * mid - dst[z, tile(i), :] + m_x[z, tile(i), :] * lap
                u = u + jnp.where(cell + 1024 * i == src_cell, amount, 0.0)
                miss = jnp.where(active, hits[z - 4, inner(i), :] * u - res[t, z - 4, inner(i), :], 0.0)
                found.append((z, i, lap, u, miss))
            for z, i, lap, u, miss in found:
                laps[t, z - 4, inner(i), :] = lap
                dst[z, tile(i), :] = u
                res[t, z - 4, inner(i), :] = miss

        return body

    def fwd_pair(i, c):
        par, then = lax.rem(i, 2), lax.rem(i + 1, 2)
        step = forward(u_a, u_b, 2 * i)
        blocks(step, 12, 8, 3)

        @pl.when(i == 0)
        def _():
            model_halo[2](put(m_x, land_m, 8))
            model_halo[1]()

        u_halo(par)[2](put(u_a, land.at[par], 8))
        blocks(step, 4, 32, 2)
        u_halo(par)[1]()
        step = forward(u_b, u_a, 2 * i + 1)
        blocks(step, 8, 24, 2)
        pl.when(i < STEPS // 2 - 1)(u_halo(then)[0])
        blocks(step, 16, 8, 2)
        return c

    lax.fori_loop(0, 2, fwd_pair, 0)
    for f, dst in ((2, p_a), (3, p_p)):
        finish(fields[f], fields_own[f])
        relayout(f, dst)
    prev_halo = halo(p_p, 4, land_p.at[1], hp_s.at[1], hp_r.at[1])
    prev_halo[0]()
    lax.fori_loop(2, STEPS // 2, fwd_pair, 0)
    prev_halo[2](put(p_p, land_p.at[1], 4))
    prev_halo[1]()

    def p_halo(par):
        return halo(p_a, 8, land.at[par], h_s.at[par], h_r.at[par])

    def first(z, c):
        active = steps > STEPS - 1
        found = []
        for i in range(4):
            hit = p_a[z, tile(i), :] + res[STEPS - 1, z - 4, inner(i), :]
            part = jnp.where(active, hit * laps[STEPS - 1, z - 4, inner(i), :], 0.0)
            found.append((i, hit, m_x[z, tile(i), :] * hit, part))
        for i, hit, w, part in found:
            p_a[z, tile(i), :] = hit
            w_a[z, tile(i), :] = w
            grad[z - 4, inner(i), :] = part
        return c

    lax.fori_loop(8, 16, first, 0)
    lax.fori_loop(32, 40, first, 0)
    p_halo(0)[0]()
    lax.fori_loop(16, 32, first, 0)

    def clear_ends(z, c):
        grad[z] = jnp.zeros((32, 128), F32)
        grad[36 + z] = jnp.zeros((32, 128), F32)
        return c

    lax.fori_loop(0, 4, clear_ends, 0)

    def backward(src, dst, p_now, p_then, t):
        def body(z0):
            active, then = steps > t, steps > t - 1
            found = []
            for z, i, _, lap in stencil(src, z0, weights[...]):
                hit = p_now[z, tile(i), :]
                prev = p_p[z, tile(i), :]
                cur = jnp.where(active, 2.0 * hit - prev + lap, hit)
                prev = jnp.where(active, hit, prev)
                hit = cur + res[t - 1, z - 4, inner(i), :]
                part = jnp.where(then, hit * laps[t - 1, z - 4, inner(i), :], 0.0)
                found.append((z, i, prev, hit, m_x[z, tile(i), :] * hit, grad[z - 4, inner(i), :] + part))
            for z, i, prev, hit, w, total in found:
                p_p[z, tile(i), :] = prev
                p_then[z, tile(i), :] = hit
                dst[z, tile(i), :] = w
                grad[z - 4, inner(i), :] = total

        return body

    def adj_ends(land_ref, t):
        stepped = steps > t + 1

        def use(side, at):
            near = at + 4 * (1 - side)

            def keep(z, c):
                for i in range(4):
                    p_p[z, tile(i), :] = jnp.where(stepped, p_b[z, tile(i), :], p_p[z, tile(i), :])
                return c

            lax.fori_loop(near, near + 4, keep, 0)

            def body(z, c):
                hit = land_ref[side, z]
                p_a[at + z, pl.ds(8, 32), :] = hit
                w_a[at + z, pl.ds(8, 32), :] = m_x[at + z, pl.ds(8, 32), :] * hit
                return c

            lax.fori_loop(0, 8, body, 0)

        return use

    def adj_pair(i, c):
        par, then = lax.rem(i, 2), lax.rem(i + 1, 2)
        t = STEPS - 1 - 2 * i
        step = backward(w_a, w_b, p_a, p_b, t)
        blocks(step, 12, 8, 3)
        p_halo(par)[2](adj_ends(land.at[par], t))
        blocks(step, 4, 32, 2)
        p_halo(par)[1]()

        @pl.when(i < STEPS // 2 - 1)
        def _():
            step = backward(w_b, w_a, p_b, p_a, t - 1)
            blocks(step, 8, 24, 2)
            p_halo(then)[0]()
            blocks(step, 16, 8, 2)

        return c

    lax.fori_loop(0, STEPS // 2, adj_pair, 0)

    g_flat = grad.reshape(40 * 32, 128)

    def gather(k, c):
        for xp in range(2):
            for g in range(4):
                g_1[k, xp, pl.ds(8 * g, 8), :] = g_flat[pl.ds((4 + 8 * g) * 32 + xp + 2 * k, 8, stride=32), :]
        return c

    lax.fori_loop(0, 16, gather, 0)

    def turn(col, c):
        g_send[col] = g_1[(col - base_x) & 15]
        return c

    lax.fori_loop(0, 16, turn, 0)
    gd = over_dom(lambda p: g_send.at[p], g_t.at[:, z_of(d), :], lambda o: gd_s.at[o], lambda o: gd_r.at[o])
    gd_own = pltpu.make_async_copy(g_send.at[d], g_t.at[:, z_of(d), :], own_sem.at[7])
    start(gd, gd_own)
    finish(gd, gd_own)

    def back(q, c):
        cols = pl.ds(pl.multiple_of(q * 128, 128), 128)
        for xp in range(2):
            g_b[pl.ds(2 * xp, 2), :, cols] = g_t[xp, pl.ds(q * 128, 128), :].T.reshape(2, 64, 128)
        return c

    lax.fori_loop(0, 4, back, 0)
    gf = over_shot(lambda p: g_b.at[:, rows_of(p), :], g_recv.at[s], lambda o: gf_s.at[o], lambda o: gf_r.at[o])
    gf_own = pltpu.make_async_copy(g_b.at[:, rows_of(s), :], g_recv.at[s], own_sem.at[8])
    start(gf, gf_own)
    finish(gf, gf_own)
    owners = [jnp.full((8, 128), slot_of(shot, d), jnp.int32) for shot in range(SHOTS)]

    def add_up(slot, c):
        mine = [owner == slot for owner in owners]
        sums = []
        for x in range(4):
            for q in range(4):
                total = jnp.zeros((8, 128), F32)
                for shot in range(SHOTS):
                    total = total + jnp.where(mine[shot], g_recv[shot, x, :, pl.ds(128 * q, 128)], 0.0)
                sums.append((x, q, total))
        for x, q, total in sums:
            batch[slot, x, :, pl.ds(128 * q, 128)] = total
        return c

    lax.fori_loop(0, 16, add_up, 0)
    gg = over_shot(
        lambda p: batch.at[pl.ds(2 * p, 2)], out.at[:, :, rows_of(s), :], lambda o: gg_s.at[o], lambda o: gg_r.at[o]
    )
    gg_own = pltpu.make_async_copy(batch.at[pl.ds(2 * s, 2)], out.at[:, :, rows_of(s), :], own_sem.at[9])
    start(gg, gg_own)
    finish(gg, gg_own)


def local(
    velocity,
    fwd_prev,
    fwd_cur,
    adj_prev,
    adj_cur,
    wavelet,
    src_pos,
    rec_pos,
    observed,
    step_count,
    aperture,
    block_slot,
    prev_batch,
    snapshot,
):
    shape = (2, 4, 64, 512)
    hbm = pl.BlockSpec(memory_space=pl.ANY)
    vmem = pl.BlockSpec(memory_space=pltpu.VMEM)
    smem = pl.BlockSpec(memory_space=pltpu.SMEM)
    field = pltpu.VMEM((PLANES, ROWS, 128), F32)
    dma = pltpu.SemaphoreType.DMA
    scratch = [
        pltpu.VMEM((16, 4, 8, 512), F32),
        pltpu.VMEM((8, 4, 8, 512), F32),
        pltpu.VMEM((4, 64, 512), F32),
        pltpu.VMEM((2, 512, 128), F32),
        pltpu.VMEM((16, 2, 32, 128), F32),
        pltpu.VMEM((4, 4, 64, 512), F32),
        pltpu.VMEM((4, 2, 512, 128), F32),
        pltpu.VMEM((4, 32, 32, 128), F32),
        *[field] * 8,
        pltpu.VMEM((STEPS, 40, 32, 128), F32),
        pltpu.VMEM((STEPS, 40, 32, 128), F32),
        pltpu.VMEM((40, 32, 128), F32),
        pltpu.VMEM((5, 256, 256), jnp.bfloat16),
        pltpu.VMEM((256, 256), jnp.bfloat16),
        pltpu.VMEM((40, 32, 128), F32),
        pltpu.VMEM((2, 2, 8, 32, 128), F32),
        pltpu.VMEM((2, 8, 32, 128), F32),
        pltpu.VMEM((2, 2, 4, 32, 128), F32),
        pltpu.VMEM((16, 2, 32, 128), F32),
        pltpu.VMEM((16, 2, 32, 128), F32),
        pltpu.VMEM((2, 512, 128), F32),
        pltpu.VMEM((4, 64, 512), F32),
        pltpu.VMEM((8, 4, 8, 512), F32),
        pltpu.VMEM((16, 4, 8, 512), F32),
        dma((4,)),
        dma((10,)),
        dma((8,)), dma((8,)),
        dma((4, 16)), dma((4, 16)),
        dma((8,)), dma((8,)),
        dma((16,)), dma((16,)),
        dma((16,)), dma((16,)),
        dma((8,)), dma((8,)),
        dma((8,)), dma((8,)),
        dma((2, 2)), dma((2, 2)),
        dma((2,)), dma((2,)),
        dma((2, 2)), dma((2, 2)),
    ]
    batch = pl.pallas_call(
        kernel,
        out_shape=jax.ShapeDtypeStruct(shape, F32),
        in_specs=[hbm] * 5 + [vmem] * 2 + [smem] * 5,
        out_specs=hbm,
        scratch_shapes=scratch,
        name="adjoint_gradient",
        compiler_params=pltpu.CompilerParams(collective_id=0, has_side_effects=True, vmem_limit_bytes=56 << 20),
    )(
        velocity.reshape(shape),
        fwd_cur[0],
        fwd_prev[0],
        adj_cur[0],
        adj_prev[0],
        rec_pos,
        observed[0],
        wavelet[0],
        src_pos,
        step_count,
        aperture,
        block_slot,
    )
    result = (batch - prev_batch.reshape(shape)) + snapshot.reshape(shape)
    return result.reshape(velocity.shape)


def solution(mesh):
    placed = (
        P("shot", "dom", None, None, None),
        P("shot", "dom", None, None),
        P("shot", "dom", None, None),
        P("shot", "dom", None, None),
        P("shot", "dom", None, None),
        P("shot", None),
        P("shot"),
        P("shot", None),
        P("shot", None, None),
        P("shot"),
        P(),
        P(),
        P("shot", "dom", None, None, None),
        P("shot", "dom", None, None, None),
    )
    return jax.shard_map(
        local,
        mesh=mesh,
        in_specs=placed,
        out_specs=P("shot", "dom", None, None, None),
        check_vma=False,
    )
```

time: 213 us -> 136 us (0.64)
  Pallas kernels: 206 us -> 131 us
    pallas_call x1, Pallas kernels: 206 us -> 131 us  [local(): pl.pallas_call(kernel, out_shape=jax.ShapeDtypeStruct(shape, F32), in_spe...]
where the time goes in v2:
time: 136 us; the launch traced here: 135 us
  Pallas kernels  131 us (96%)
  other arithmetic  2.54 us (2%)
    pallas_call x1, Pallas kernels, local(): pl.pallas_call(kernel, out_shape=jax.ShapeDtypeStruct(shape, F32), in_spe...  131 us

profile of v2, /device:TPU:0, one launch (start us, length us, event | category | flops | bytes accessed | tf_op | source)
XLA Modules:
  0.0 134.6 jit_solution(18068192080977706726)
XLA Ops:
  1.3 0.0 copy-start
  1.3 0.0 copy-start.1
  1.3 130.7 %adjoint_gradient.1 = f32[2,4,64,512]{3,2,1,0:T(8,128)} custom-call(f32[2,4,64,512]{3,2,1,0:T(8,128)} %bitcast.19, f32[4,64,512]{2,1,0:T(8,128)} %bitcast.20, f32[4,64,512]{2,1,0:T(8,128)} %bitcast.21, f32[4,64,512]{2,1,0:T(8,128)} %bitcast.22, f32[4,64,512]{2,1,0:T(8,128)} %bitcast.23, s32[1,256]{1,0:T(1,128)} %rec_pos.1, f32[8,256]{1,0:T(8,128)} %bitcast.24, ...), custom_call_target="tpu_custom_call" | custom-call | tf_op jit(solution)/shard_map/adjoint_gradient/pallas_call | solution.py:583
  132.0 0.0 copy-done
  132.0 0.0 copy-done.1
  132.0 2.5 %fusion = f32[2,1,4,64,512]{4,3,2,1,0:T(8,128)} fusion(f32[2,1,4,64,512]{4,3,2,1,0:T(8,128)S(1)} %copy-done, f32[2,4,64,512]{3,2,1,0:T(8,128)} %adjoint_gradient.1, f32[2,1,4,64,512]{4,3,2,1,0:T(8,128)S(1)} %copy-done.1), kind=kLoop, calls=%fused_computation.1 | loop fusion | flops 524288 | bytes 4194304 | tf_op jit(solution)/shard_map/reshape | solution.py:606
Async XLA Ops:
  1.3 130.7 %copy-start = (f32[2,1,4,64,512]{4,3,2,1,0:T(8,128)S(1)}, f32[2,1,4,64,512]{4,3,2,1,0:T(8,128)}, u32[]{:S(2)}) copy-start(f32[2,1,4,64,512]{4,3,2,1,0:T(8,128)} %param.27) | copy-start | bytes 3145732
  1.3 130.7 %copy-start.1 = (f32[2,1,4,64,512]{4,3,2,1,0:T(8,128)S(1)}, f32[2,1,4,64,512]{4,3,2,1,0:T(8,128)}, u32[]{:S(2)}) copy-start(f32[2,1,4,64,512]{4,3,2,1,0:T(8,128)} %param.26) | copy-start | bytes 3145732

commit v3 on v2

--- a/solution.py
+++ b/solution.py
@@ -66,6 +66,7 @@
 ):
     s, d = lax.axis_index("shot"), lax.axis_index("dom")
     e = chunk_of(d)
+    x, half_id = s // 2, lax.rem(s, 2)
 
     loads = []
     for f, ref in enumerate((fwd_cur, fwd_prev, adj_cur, adj_prev)):
@@ -78,9 +79,12 @@
     for o in range(1, SHOTS):
         pl.semaphore_signal(barrier, inc=1, device_id=(lax.rem(s + o, SHOTS), d), device_id_type=MESH)
 
+    def partner(o):
+        return lax.rem(d // 8 + o // 8, 2) * 8 + lax.rem(d + o, 8)
+
     def over_dom(src, dst, send, recv):
         def copy(o):
-            p = lax.rem(d + o, DOM)
+            p = partner(o)
             return pltpu.make_async_remote_copy(
                 src_ref=src(p), dst_ref=dst, send_sem=send(o), recv_sem=recv(o), device_id=(s, p), device_id_type=MESH
             )
@@ -96,11 +100,20 @@
 
         return copy, SHOTS
 
+    def over_x(src, dst, send, recv):
+        def copy(o):
+            p = lax.rem(s + 2 * o, SHOTS)
+            return pltpu.make_async_remote_copy(
+                src_ref=src(p), dst_ref=dst, send_sem=send(o), recv_sem=recv(o), device_id=(p, d), device_id_type=MESH
+            )
+
+        return copy, SHOTS // 2
+
     def start(exchange, own):
         copy, n = exchange
 
         def body(o, c):
-            copy(o).start()
+            copy(n - o).start()
             return c
 
         lax.fori_loop(1, n, body, 0)
@@ -116,28 +129,32 @@
         lax.fori_loop(1, n, body, 0)
         own.wait()
 
+    def transpose_pair(src, dst, xp):
+        def body(q, c):
+            block = src[pl.ds(2 * xp, 2), :, pl.ds(pl.multiple_of(q * 128, 128), 128)]
+            dst[xp, pl.ds(q * 128, 128), :] = block.reshape(128, 128).T
+            return c
+
+        lax.fori_loop(0, 4, body, 0)
+
     def transpose_in(src, dst):
-        def body(q, c):
-            for xp in range(2):
-                block = src[pl.ds(2 * xp, 2), :, pl.ds(pl.multiple_of(q * 128, 128), 128)]
-                dst[xp, pl.ds(q * 128, 128), :] = block.reshape(128, 128).T
-            return c
-
-        lax.fori_loop(0, 4, body, 0)
+        for xp in range(2):
+            transpose_pair(src, dst, xp)
 
     def z_of(p):
         return pl.ds(chunk_of(p) * 32, 32)
 
     def rows_of(p):
         return pl.ds(p * 8, 8)
+
+    def quarter(p):
+        return pl.ds((p // 2) * 16, 16)
 
     loads[0].wait()
     transpose_in(f_in.at[0], f_t.at[0])
     pl.semaphore_wait(barrier, DOM + SHOTS - 2)
-    va = over_shot(
-        lambda p: vel.at[:, :, rows_of(p), :], v_2.at[pl.ds(2 * s, 2)], lambda o: va_s.at[o], lambda o: va_r.at[o]
-    )
-    va_own = pltpu.make_async_copy(vel.at[:, :, rows_of(s), :], v_2.at[pl.ds(2 * s, 2)], own_sem.at[0])
+    va = over_x(lambda p: vel.at[:, :, quarter(p), :], v_2.at[pl.ds(2 * x, 2)], lambda o: va_s.at[o], lambda o: va_r.at[o])
+    va_own = pltpu.make_async_copy(vel.at[:, :, quarter(s), :], v_2.at[pl.ds(2 * x, 2)], own_sem.at[0, 0])
     start(va, va_own)
 
     fields, fields_own = [], []
@@ -150,7 +167,7 @@
                 lambda o, f=f: f_r.at[f, o],
             )
         )
-        fields_own.append(pltpu.make_async_copy(f_t.at[f, :, z_of(d), :], f_1.at[f, pl.ds(2 * d, 2)], own_sem.at[1 + f]))
+        fields_own.append(pltpu.make_async_copy(f_t.at[f, :, z_of(d), :], f_1.at[f, pl.ds(2 * d, 2)], own_sem.at[1 + f, 0]))
     start(fields[0], fields_own[0])
     loads[1].wait()
     transpose_in(f_in.at[1], f_t.at[1])
@@ -159,6 +176,19 @@
         loads[f].wait()
         transpose_in(f_in.at[f], f_t.at[f])
 
+    def send_adjoint(lo, hi):
+        for f in range(2, 4):
+
+            def body(o, c, f=f):
+                fields[f][0](o).start()
+                return c
+
+            lax.fori_loop(lo, hi, body, 0)
+
+    for f in range(2, 4):
+        fields_own[f].start()
+    send_adjoint(8, 10)
+
     pos = rec_pos[...]
     rec_row = (((pos & 511) - 32 * e + 4) << 5) + (pos >> 16)
     rec_lane = (((pos >> 15) & 1) << 6) + ((pos >> 9) & 63)
@@ -193,21 +223,25 @@
     lax.fori_loop(0, PLANES, clear, 0)
     weights[...] = band()
 
-    finish(va, va_own)
-
     def slot_of(shot, col):
         first = aperture[shot, 0]
         block_x = (first >> 3) + ((col - (first >> 3)) & 15)
         return block_slot[((block_x >> 4) << 3) + (first & 7)]
 
+    finish(va, va_own)
+
     def pick(shot, c):
-        picks[shot] = v_2[slot_of(shot, d)]
+        slot = slot_of(shot, d)
+        picks[shot] = v_2[((slot >> 2) << 1) + (slot & 1)]
         return c
 
     lax.fori_loop(0, SHOTS, pick, 0)
-    vb = over_shot(lambda p: picks.at[p], m_b.at[:, rows_of(s), :], lambda o: vb_s.at[o], lambda o: vb_r.at[o])
-    vb_own = pltpu.make_async_copy(picks.at[s], m_b.at[:, rows_of(s), :], own_sem.at[5])
+    offer = m_b.at[half_id, :, quarter(s), :]
+    vb = over_shot(lambda p: picks.at[p], offer, lambda o: vb_s.at[o], lambda o: vb_r.at[o])
+    vb_own = pltpu.make_async_copy(picks.at[s], offer, own_sem.at[5, 0])
     start(vb, vb_own)
+    send_adjoint(1, 8)
+    send_adjoint(10, 12)
 
     def relayout(f, dst):
         flat = dst.reshape(PLANES * ROWS, 128)
@@ -286,15 +320,24 @@
     prev_halo[0]()
 
     finish(vb, vb_own)
-    transpose_in(m_b, m_t)
+    in_first = (jnp.full((128, 128), slot_of(s, d), jnp.int32) & 2) == 0
+
+    def choose(q, c):
+        cols = pl.ds(pl.multiple_of(q * 128, 128), 128)
+        for xp in range(2):
+            two = [m_b[half, pl.ds(2 * xp, 2), :, cols].reshape(128, 128) for half in range(2)]
+            m_t[xp, pl.ds(q * 128, 128), :] = jnp.where(in_first, two[0], two[1]).T
+        return c
+
+    lax.fori_loop(0, 4, choose, 0)
     vc = over_dom(lambda p: m_t.at[:, z_of(p), :], m_1.at[d], lambda o: vc_s.at[o], lambda o: vc_r.at[o])
-    vc_own = pltpu.make_async_copy(m_t.at[:, z_of(d), :], m_1.at[d], own_sem.at[6])
+    vc_own = pltpu.make_async_copy(m_t.at[:, z_of(d), :], m_1.at[d], own_sem.at[6, 0])
     start(vc, vc_own)
+
+    send_adjoint(12, 14)
     prev_halo[2](put(u_b, land_p.at[0], 4))
     prev_halo[1]()
     finish(vc, vc_own)
-    for f in range(2, 4):
-        start(fields[f], fields_own[f])
     m_flat = m_x.reshape(PLANES * ROWS, 128)
     base_x = aperture[s, 0] >> 3
 
@@ -360,19 +403,16 @@
         u_halo(par)[1]()
         step = forward(u_b, u_a, 2 * i + 1)
         blocks(step, 8, 24, 2)
+
         pl.when(i < STEPS // 2 - 1)(u_halo(then)[0])
+        pl.when(i == 0)(functools.partial(send_adjoint, 14, 16))
+
         blocks(step, 16, 8, 2)
         return c
 
-    lax.fori_loop(0, 2, fwd_pair, 0)
-    for f, dst in ((2, p_a), (3, p_p)):
-        finish(fields[f], fields_own[f])
-        relayout(f, dst)
-    prev_halo = halo(p_p, 4, land_p.at[1], hp_s.at[1], hp_r.at[1])
-    prev_halo[0]()
-    lax.fori_loop(2, STEPS // 2, fwd_pair, 0)
-    prev_halo[2](put(p_p, land_p.at[1], 4))
-    prev_halo[1]()
+    lax.fori_loop(0, STEPS // 2, fwd_pair, 0)
+    finish(fields[2], fields_own[2])
+    relayout(2, p_a)
 
     def p_halo(par):
         return halo(p_a, 8, land.at[par], h_s.at[par], h_r.at[par])
@@ -393,6 +433,10 @@
     lax.fori_loop(8, 16, first, 0)
     lax.fori_loop(32, 40, first, 0)
     p_halo(0)[0]()
+    finish(fields[3], fields_own[3])
+    relayout(3, p_p)
+    adj_prev_halo = halo(p_p, 4, land_p.at[1], hp_s.at[1], hp_r.at[1])
+    adj_prev_halo[0]()
     lax.fori_loop(16, 32, first, 0)
 
     def clear_ends(z, c):
@@ -449,7 +493,13 @@
         par, then = lax.rem(i, 2), lax.rem(i + 1, 2)
         t = STEPS - 1 - 2 * i
         step = backward(w_a, w_b, p_a, p_b, t)
+        pl.when(i == 0)(adj_prev_halo[1])
         blocks(step, 12, 8, 3)
+
+        @pl.when(i == 0)
+        def _():
+            adj_prev_halo[2](put(p_p, land_p.at[1], 4))
+
         p_halo(par)[2](adj_ends(land.at[par], t))
         blocks(step, 4, 32, 2)
         p_halo(par)[1]()
@@ -467,57 +517,87 @@
 
     g_flat = grad.reshape(40 * 32, 128)
 
-    def gather(k, c):
-        for xp in range(2):
+    gd, gd_own = [], []
+    for h in range(2):
+
+        def gather(k, c, h=h):
             for g in range(4):
-                g_1[k, xp, pl.ds(8 * g, 8), :] = g_flat[pl.ds((4 + 8 * g) * 32 + xp + 2 * k, 8, stride=32), :]
-        return c
-
-    lax.fori_loop(0, 16, gather, 0)
-
-    def turn(col, c):
-        g_send[col] = g_1[(col - base_x) & 15]
-        return c
-
-    lax.fori_loop(0, 16, turn, 0)
-    gd = over_dom(lambda p: g_send.at[p], g_t.at[:, z_of(d), :], lambda o: gd_s.at[o], lambda o: gd_r.at[o])
-    gd_own = pltpu.make_async_copy(g_send.at[d], g_t.at[:, z_of(d), :], own_sem.at[7])
-    start(gd, gd_own)
-    finish(gd, gd_own)
-
-    def back(q, c):
-        cols = pl.ds(pl.multiple_of(q * 128, 128), 128)
-        for xp in range(2):
-            g_b[pl.ds(2 * xp, 2), :, cols] = g_t[xp, pl.ds(q * 128, 128), :].T.reshape(2, 64, 128)
-        return c
-
-    lax.fori_loop(0, 4, back, 0)
-    gf = over_shot(lambda p: g_b.at[:, rows_of(p), :], g_recv.at[s], lambda o: gf_s.at[o], lambda o: gf_r.at[o])
-    gf_own = pltpu.make_async_copy(g_b.at[:, rows_of(s), :], g_recv.at[s], own_sem.at[8])
-    start(gf, gf_own)
-    finish(gf, gf_own)
+                g_1[h, k, pl.ds(8 * g, 8), :] = g_flat[pl.ds((4 + 8 * g) * 32 + h + 2 * k, 8, stride=32), :]
+            return c
+
+        lax.fori_loop(0, 16, gather, 0)
+
+        def turn(col, c, h=h):
+            g_send[h, col] = g_1[h, (col - base_x) & 15]
+            return c
+
+        lax.fori_loop(0, 16, turn, 0)
+        gd.append(
+            over_dom(
+                lambda p, h=h: g_send.at[h, p],
+                g_t.at[h, z_of(d), :],
+                lambda o, h=h: gd_s.at[h, o],
+                lambda o, h=h: gd_r.at[h, o],
+            )
+        )
+        gd_own.append(pltpu.make_async_copy(g_send.at[h, d], g_t.at[h, z_of(d), :], own_sem.at[7, h]))
+        start(gd[h], gd_own[h])
+
+    gf, gf_own = [], []
+    for h in range(2):
+        finish(gd[h], gd_own[h])
+        half = pl.ds(2 * h, 2)
+
+        def back(q, c, h=h, half=half):
+            cols = pl.ds(pl.multiple_of(q * 128, 128), 128)
+            g_b[half, :, cols] = g_t[h, pl.ds(q * 128, 128), :].T.reshape(2, 64, 128)
+            return c
+
+        lax.fori_loop(0, 4, back, 0)
+        gf.append(
+            over_shot(
+                lambda p, half=half: g_b.at[half, rows_of(p), :],
+                g_recv.at[h, s],
+                lambda o, h=h: gf_s.at[h, o],
+                lambda o, h=h: gf_r.at[h, o],
+            )
+        )
+        gf_own.append(pltpu.make_async_copy(g_b.at[half, rows_of(s), :], g_recv.at[h, s], own_sem.at[8, h]))
+        start(gf[h], gf_own[h])
+
     owners = [jnp.full((8, 128), slot_of(shot, d), jnp.int32) for shot in range(SHOTS)]
-
-    def add_up(slot, c):
-        mine = [owner == slot for owner in owners]
-        sums = []
-        for x in range(4):
-            for q in range(4):
-                total = jnp.zeros((8, 128), F32)
-                for shot in range(SHOTS):
-                    total = total + jnp.where(mine[shot], g_recv[shot, x, :, pl.ds(128 * q, 128)], 0.0)
-                sums.append((x, q, total))
-        for x, q, total in sums:
-            batch[slot, x, :, pl.ds(128 * q, 128)] = total
-        return c
-
-    lax.fori_loop(0, 16, add_up, 0)
-    gg = over_shot(
-        lambda p: batch.at[pl.ds(2 * p, 2)], out.at[:, :, rows_of(s), :], lambda o: gg_s.at[o], lambda o: gg_r.at[o]
-    )
-    gg_own = pltpu.make_async_copy(batch.at[pl.ds(2 * s, 2)], out.at[:, :, rows_of(s), :], own_sem.at[9])
-    start(gg, gg_own)
-    finish(gg, gg_own)
+    gg, gg_own = [], []
+    for h in range(2):
+        finish(gf[h], gf_own[h])
+        half = pl.ds(2 * h, 2)
+
+        def add_up(slot, c, h=h):
+            mine = [owner == slot for owner in owners]
+            sums = []
+            for x in range(2):
+                for q in range(4):
+                    total = jnp.zeros((8, 128), F32)
+                    for shot in range(SHOTS):
+                        total = total + jnp.where(mine[shot], g_recv[h, shot, x, :, pl.ds(128 * q, 128)], 0.0)
+                    sums.append((x, q, total))
+            for x, q, total in sums:
+                batch[h, slot, x, :, pl.ds(128 * q, 128)] = total
+            return c
+
+        lax.fori_loop(0, 16, add_up, 0)
+        target = out.at[:, half, rows_of(s), :]
+        gg.append(
+            over_shot(
+                lambda p, h=h: batch.at[h, pl.ds(2 * p, 2)],
+                target,
+                lambda o, h=h: gg_s.at[h, o],
+                lambda o, h=h: gg_r.at[h, o],
+            )
+        )
+        gg_own.append(pltpu.make_async_copy(batch.at[h, pl.ds(2 * s, 2)], target, own_sem.at[9, h]))
+        start(gg[h], gg_own[h])
+    for h in range(2):
+        finish(gg[h], gg_own[h])
 
 
 def local(
@@ -543,9 +623,9 @@
     field = pltpu.VMEM((PLANES, ROWS, 128), F32)
     dma = pltpu.SemaphoreType.DMA
     scratch = [
-        pltpu.VMEM((16, 4, 8, 512), F32),
-        pltpu.VMEM((8, 4, 8, 512), F32),
-        pltpu.VMEM((4, 64, 512), F32),
+        pltpu.VMEM((8, 4, 16, 512), F32),
+        pltpu.VMEM((8, 4, 16, 512), F32),
+        pltpu.VMEM((2, 4, 64, 512), F32),
         pltpu.VMEM((2, 512, 128), F32),
         pltpu.VMEM((16, 2, 32, 128), F32),
         pltpu.VMEM((4, 4, 64, 512), F32),
@@ -561,21 +641,21 @@
         pltpu.VMEM((2, 2, 8, 32, 128), F32),
         pltpu.VMEM((2, 8, 32, 128), F32),
         pltpu.VMEM((2, 2, 4, 32, 128), F32),
-        pltpu.VMEM((16, 2, 32, 128), F32),
-        pltpu.VMEM((16, 2, 32, 128), F32),
+        pltpu.VMEM((2, 16, 32, 128), F32),
+        pltpu.VMEM((2, 16, 32, 128), F32),
         pltpu.VMEM((2, 512, 128), F32),
         pltpu.VMEM((4, 64, 512), F32),
-        pltpu.VMEM((8, 4, 8, 512), F32),
-        pltpu.VMEM((16, 4, 8, 512), F32),
+        pltpu.VMEM((2, 8, 2, 8, 512), F32),
+        pltpu.VMEM((2, 16, 2, 8, 512), F32),
         dma((4,)),
-        dma((10,)),
-        dma((8,)), dma((8,)),
+        dma((10, 2)),
+        dma((4,)), dma((4,)),
         dma((4, 16)), dma((4, 16)),
         dma((8,)), dma((8,)),
         dma((16,)), dma((16,)),
-        dma((16,)), dma((16,)),
-        dma((8,)), dma((8,)),
-        dma((8,)), dma((8,)),
+        dma((2, 16)), dma((2, 16)),
+        dma((2, 8)), dma((2, 8)),
+        dma((2, 8)), dma((2, 8)),
         dma((2, 2)), dma((2, 2)),
         dma((2,)), dma((2,)),
         dma((2, 2)), dma((2, 2)),

time: 136 us -> 123 us (0.904); the launches traced: 135 us -> 123 us
  Pallas kernels: 131 us -> 119 us
    pallas_call x1, Pallas kernels: 131 us -> 119 us  [local(): pl.pallas_call(kernel, out_shape=jax.ShapeDtypeStruct(shape, F32), in_spe...]
where the time goes in v3:
time: 123 us
  Pallas kernels  119 us (97%)
  other arithmetic  2.54 us (2%)
  between operations  1.34 us (1%)
    pallas_call x1, Pallas kernels, local(): pl.pallas_call(kernel, out_shape=jax.ShapeDtypeStruct(shape, F32), in_spe...  119 us
    reshape x1, other arithmetic, local(): return result.reshape(velocity.shape)  2.54 us

profile of v3, /device:TPU:0, one launch (start us, length us, event | category | flops | bytes accessed | tf_op | source)
XLA Modules:
  0.0 123.2 jit_solution(2048864854562779477)
XLA Ops:
  1.3 0.0 copy-start
  1.3 0.0 copy-start.1
  1.3 119.3 %adjoint_gradient.1 = f32[2,4,64,512]{3,2,1,0:T(8,128)} custom-call(f32[2,4,64,512]{3,2,1,0:T(8,128)} %bitcast.19, f32[4,64,512]{2,1,0:T(8,128)} %bitcast.20, f32[4,64,512]{2,1,0:T(8,128)} %bitcast.21, f32[4,64,512]{2,1,0:T(8,128)} %bitcast.22, f32[4,64,512]{2,1,0:T(8,128)} %bitcast.23, s32[1,256]{1,0:T(1,128)} %rec_pos.1, f32[8,256]{1,0:T(8,128)} %bitcast.24, ...), custom_call_target="tpu_custom_call" | custom-call | tf_op jit(solution)/shard_map/adjoint_gradient/pallas_call | solution.py:663
  120.6 0.0 copy-done
  120.6 0.0 copy-done.1
  120.6 2.5 %fusion = f32[2,1,4,64,512]{4,3,2,1,0:T(8,128)} fusion(f32[2,1,4,64,512]{4,3,2,1,0:T(8,128)S(1)} %copy-done, f32[2,4,64,512]{3,2,1,0:T(8,128)} %adjoint_gradient.1, f32[2,1,4,64,512]{4,3,2,1,0:T(8,128)S(1)} %copy-done.1), kind=kLoop, calls=%fused_computation.1 | loop fusion | flops 524288 | bytes 4194304 | tf_op jit(solution)/shard_map/reshape | solution.py:686
Async XLA Ops:
  1.3 119.3 %copy-start = (f32[2,1,4,64,512]{4,3,2,1,0:T(8,128)S(1)}, f32[2,1,4,64,512]{4,3,2,1,0:T(8,128)}, u32[]{:S(2)}) copy-start(f32[2,1,4,64,512]{4,3,2,1,0:T(8,128)} %param.27) | copy-start | bytes 3145732
  1.3 119.3 %copy-start.1 = (f32[2,1,4,64,512]{4,3,2,1,0:T(8,128)S(1)}, f32[2,1,4,64,512]{4,3,2,1,0:T(8,128)}, u32[]{:S(2)}) copy-start(f32[2,1,4,64,512]{4,3,2,1,0:T(8,128)} %param.26) | copy-start | bytes 3145732

commit v4 on v3

--- a/solution.py
+++ b/solution.py
@@ -24,7 +24,7 @@
     col = lax.broadcasted_iota(jnp.int32, (256, 256), 1)
     gap = jnp.abs((row & 127) - (col & 127))
     same = ((row >> 6) & 1) == ((col >> 6) & 1)
-    full = jnp.zeros((256, 256), F32)
+    full = jnp.where(same & (gap == 0), 3.0 * C0, 0.0)
     for k, c in ((1, C1), (2, C2), (3, C3), (4, C4)):
         full = full + jnp.where(same & (gap == k), c, 0.0)
     high = full.astype(jnp.bfloat16).astype(F32)
@@ -50,7 +50,7 @@
             pairs[3] = pairs[3] + (up2 + dn2)
             odd = C1 * (jnp.where(low, up1, mid) + jnp.where(low, mid, dn1))
             odd = odd + C3 * (jnp.where(low, up2, up1) + jnp.where(low, dn1, dn2))
-            total = (3.0 * C0) * mid + C1 * pairs[0] + C2 * pairs[1] + C3 * pairs[2] + C4 * pairs[3]
+            total = C1 * pairs[0] + C2 * pairs[1] + C3 * pairs[2] + C4 * pairs[3]
             lap = total + pltpu.roll(odd, 64, 1) + along_y[32 * p + 8 * i : 32 * p + 8 * i + 8]
             yield z, i, mid, lap
 
@@ -58,7 +58,7 @@
 def kernel(
     vel, fwd_cur, fwd_prev, adj_cur, adj_prev, rec_pos, observed, wavelet, src_pos, count, aperture, block_slot,
     out,
-    v_2, picks, m_b, m_t, m_1, f_in, f_t, f_1,
+    v_2a, v_2b, picks, m_b, m_t, m_1, f_in, f_t, f_1,
     u_a, u_b, p_a, p_b, p_p, w_a, w_b, m_x, laps, res, hits, onehot, weights, grad, land, land_m, land_p,
     g_1, g_send, g_t, g_b, g_recv, batch,
     in_sem, own_sem, va_s, va_r, f_s, f_r, vb_s, vb_r, vc_s, vc_r, gd_s, gd_r, gf_s, gf_r, gg_s, gg_r,
@@ -112,11 +112,11 @@
     def start(exchange, own):
         copy, n = exchange
 
-        def body(o, c):
-            copy(n - o).start()
-            return c
-
-        lax.fori_loop(1, n, body, 0)
+        def body(k, c):
+            copy(2 * k - 1 - 7 * (k // 5) if n == SHOTS else n - k).start()
+            return c
+
+        lax.fori_loop(1, n, body, 0, unroll=True)
         own.start()
 
     def finish(exchange, own):
@@ -126,7 +126,7 @@
             copy(o).wait()
             return c
 
-        lax.fori_loop(1, n, body, 0)
+        lax.fori_loop(1, n, body, 0, unroll=True)
         own.wait()
 
     def transpose_pair(src, dst, xp):
@@ -153,9 +153,20 @@
     loads[0].wait()
     transpose_in(f_in.at[0], f_t.at[0])
     pl.semaphore_wait(barrier, DOM + SHOTS - 2)
-    va = over_x(lambda p: vel.at[:, :, quarter(p), :], v_2.at[pl.ds(2 * x, 2)], lambda o: va_s.at[o], lambda o: va_r.at[o])
-    va_own = pltpu.make_async_copy(vel.at[:, :, quarter(s), :], v_2.at[pl.ds(2 * x, 2)], own_sem.at[0, 0])
-    start(va, va_own)
+    va, va_own = [], []
+    for h in range(2):
+        half = pl.ds(2 * h, 2)
+        mine = (v_2a, v_2b)[h].at[pl.ds(2 * x, 2)]
+        va.append(
+            over_x(
+                lambda p, half=half: vel.at[:, half, quarter(p), :],
+                mine,
+                lambda o, h=h: va_s.at[h, o],
+                lambda o, h=h: va_r.at[h, o],
+            )
+        )
+        va_own.append(pltpu.make_async_copy(vel.at[:, half, quarter(s), :], mine, own_sem.at[0, h]))
+        start(va[h], va_own[h])
 
     fields, fields_own = [], []
     for f in range(4):
@@ -187,7 +198,6 @@
 
     for f in range(2, 4):
         fields_own[f].start()
-    send_adjoint(8, 10)
 
     pos = rec_pos[...]
     rec_row = (((pos & 511) - 32 * e + 4) << 5) + (pos >> 16)
@@ -228,20 +238,23 @@
         block_x = (first >> 3) + ((col - (first >> 3)) & 15)
         return block_slot[((block_x >> 4) << 3) + (first & 7)]
 
-    finish(va, va_own)
-
-    def pick(shot, c):
-        slot = slot_of(shot, d)
-        picks[shot] = v_2[((slot >> 2) << 1) + (slot & 1)]
-        return c
-
-    lax.fori_loop(0, SHOTS, pick, 0)
-    offer = m_b.at[half_id, :, quarter(s), :]
-    vb = over_shot(lambda p: picks.at[p], offer, lambda o: vb_s.at[o], lambda o: vb_r.at[o])
-    vb_own = pltpu.make_async_copy(picks.at[s], offer, own_sem.at[5, 0])
-    start(vb, vb_own)
+    vb, vb_own = [], []
+    for h in range(2):
+        finish(va[h], va_own[h])
+
+        def pick(shot, c, h=h):
+            slot = slot_of(shot, d)
+            picks[h, shot] = (v_2a, v_2b)[h][((slot >> 2) << 1) + (slot & 1)]
+            return c
+
+        lax.fori_loop(0, SHOTS, pick, 0)
+        offer = m_b.at[half_id, pl.ds(2 * h, 2), quarter(s), :]
+        vb.append(
+            over_shot(lambda p, h=h: picks.at[h, p], offer, lambda o, h=h: vb_s.at[h, o], lambda o, h=h: vb_r.at[h, o])
+        )
+        vb_own.append(pltpu.make_async_copy(picks.at[h, s], offer, own_sem.at[5, h]))
+        start(vb[h], vb_own[h])
     send_adjoint(1, 8)
-    send_adjoint(10, 12)
 
     def relayout(f, dst):
         flat = dst.reshape(PLANES * ROWS, 128)
@@ -319,25 +332,33 @@
     prev_halo = halo(u_b, 4, land_p.at[0], hp_s.at[0], hp_r.at[0])
     prev_halo[0]()
 
-    finish(vb, vb_own)
     in_first = (jnp.full((128, 128), slot_of(s, d), jnp.int32) & 2) == 0
-
-    def choose(q, c):
-        cols = pl.ds(pl.multiple_of(q * 128, 128), 128)
-        for xp in range(2):
-            two = [m_b[half, pl.ds(2 * xp, 2), :, cols].reshape(128, 128) for half in range(2)]
-            m_t[xp, pl.ds(q * 128, 128), :] = jnp.where(in_first, two[0], two[1]).T
-        return c
-
-    lax.fori_loop(0, 4, choose, 0)
-    vc = over_dom(lambda p: m_t.at[:, z_of(p), :], m_1.at[d], lambda o: vc_s.at[o], lambda o: vc_r.at[o])
-    vc_own = pltpu.make_async_copy(m_t.at[:, z_of(d), :], m_1.at[d], own_sem.at[6, 0])
-    start(vc, vc_own)
-
-    send_adjoint(12, 14)
+    vc, vc_own = [], []
+    for h in range(2):
+        finish(vb[h], vb_own[h])
+
+        def choose(q, c, h=h):
+            cols = pl.ds(pl.multiple_of(q * 128, 128), 128)
+            two = [m_b[part, pl.ds(2 * h, 2), :, cols].reshape(128, 128) for part in range(2)]
+            m_t[h, pl.ds(q * 128, 128), :] = jnp.where(in_first, two[0], two[1]).T
+            return c
+
+        lax.fori_loop(0, 4, choose, 0)
+        vc.append(
+            over_dom(
+                lambda p, h=h: m_t.at[h, z_of(p), :],
+                m_1.at[d, h],
+                lambda o, h=h: vc_s.at[h, o],
+                lambda o, h=h: vc_r.at[h, o],
+            )
+        )
+        vc_own.append(pltpu.make_async_copy(m_t.at[h, z_of(d), :], m_1.at[d, h], own_sem.at[6, h]))
+        start(vc[h], vc_own[h])
+    send_adjoint(8, 10)
     prev_halo[2](put(u_b, land_p.at[0], 4))
     prev_halo[1]()
-    finish(vc, vc_own)
+    for h in range(2):
+        finish(vc[h], vc_own[h])
     m_flat = m_x.reshape(PLANES * ROWS, 128)
     base_x = aperture[s, 0] >> 3
 
@@ -398,21 +419,28 @@
             model_halo[2](put(m_x, land_m, 8))
             model_halo[1]()
 
+        @pl.when(i == STEPS // 2 - 1)
+        def _():
+            for f, dst in ((2, p_a), (3, p_p)):
+                finish(fields[f], fields_own[f])
+                relayout(f, dst)
+
         u_halo(par)[2](put(u_a, land.at[par], 8))
         blocks(step, 4, 32, 2)
         u_halo(par)[1]()
         step = forward(u_b, u_a, 2 * i + 1)
         blocks(step, 8, 24, 2)
 
-        pl.when(i < STEPS // 2 - 1)(u_halo(then)[0])
-        pl.when(i == 0)(functools.partial(send_adjoint, 14, 16))
+
+        @pl.when(i < STEPS // 2 - 1)
+        def _():
+            u_halo(then)[0]()
+            send_adjoint(10 + 2 * i, 12 + 2 * i)
 
         blocks(step, 16, 8, 2)
         return c
 
     lax.fori_loop(0, STEPS // 2, fwd_pair, 0)
-    finish(fields[2], fields_own[2])
-    relayout(2, p_a)
 
     def p_halo(par):
         return halo(p_a, 8, land.at[par], h_s.at[par], h_r.at[par])
@@ -433,8 +461,6 @@
     lax.fori_loop(8, 16, first, 0)
     lax.fori_loop(32, 40, first, 0)
     p_halo(0)[0]()
-    finish(fields[3], fields_own[3])
-    relayout(3, p_p)
     adj_prev_halo = halo(p_p, 4, land_p.at[1], hp_s.at[1], hp_r.at[1])
     adj_prev_halo[0]()
     lax.fori_loop(16, 32, first, 0)
@@ -623,8 +649,9 @@
     field = pltpu.VMEM((PLANES, ROWS, 128), F32)
     dma = pltpu.SemaphoreType.DMA
     scratch = [
-        pltpu.VMEM((8, 4, 16, 512), F32),
-        pltpu.VMEM((8, 4, 16, 512), F32),
+        pltpu.VMEM((8, 2, 16, 512), F32),
+        pltpu.VMEM((8, 2, 16, 512), F32),
+        pltpu.VMEM((2, 8, 2, 16, 512), F32),
         pltpu.VMEM((2, 4, 64, 512), F32),
         pltpu.VMEM((2, 512, 128), F32),
         pltpu.VMEM((16, 2, 32, 128), F32),
@@ -649,10 +676,10 @@
         pltpu.VMEM((2, 16, 2, 8, 512), F32),
         dma((4,)),
         dma((10, 2)),
-        dma((4,)), dma((4,)),
+        dma((2, 4)), dma((2, 4)),
         dma((4, 16)), dma((4, 16)),
-        dma((8,)), dma((8,)),
-        dma((16,)), dma((16,)),
+        dma((2, 8)), dma((2, 8)),
+        dma((2, 16)), dma((2, 16)),
         dma((2, 16)), dma((2, 16)),
         dma((2, 8)), dma((2, 8)),
         dma((2, 8)), dma((2, 8)),

time: 123 us -> 122 us (level)
    pallas_call x1, Pallas kernels: 119 us -> 118 us  [local(): pl.pallas_call(kernel, out_shape=jax.ShapeDtypeStruct(shape, F32), in_spe...]
where the time goes in v4:
time: 122 us
  Pallas kernels  118 us (97%)
  other arithmetic  2.54 us (2%)
  between operations  1.34 us (1%)
    pallas_call x1, Pallas kernels, local(): pl.pallas_call(kernel, out_shape=jax.ShapeDtypeStruct(shape, F32), in_spe...  118 us
    reshape x1, other arithmetic, local(): return result.reshape(velocity.shape)  2.54 us

profile of v4, /device:TPU:0, one launch (start us, length us, event | category | flops | bytes accessed | tf_op | source)
XLA Modules:
  0.0 121.6 jit_solution(18360576016052286931)
XLA Ops:
  1.3 0.0 copy-start
  1.3 0.0 copy-start.1
  1.3 117.7 %adjoint_gradient.1 = f32[2,4,64,512]{3,2,1,0:T(8,128)} custom-call(f32[2,4,64,512]{3,2,1,0:T(8,128)} %bitcast.19, f32[4,64,512]{2,1,0:T(8,128)} %bitcast.20, f32[4,64,512]{2,1,0:T(8,128)} %bitcast.21, f32[4,64,512]{2,1,0:T(8,128)} %bitcast.22, f32[4,64,512]{2,1,0:T(8,128)} %bitcast.23, s32[1,256]{1,0:T(1,128)} %rec_pos.1, f32[8,256]{1,0:T(8,128)} %bitcast.24, ...), custom_call_target="tpu_custom_call" | custom-call | tf_op jit(solution)/shard_map/adjoint_gradient/pallas_call | solution.py:690
  119.0 0.0 copy-done
  119.0 0.0 copy-done.1
  119.0 2.5 %fusion = f32[2,1,4,64,512]{4,3,2,1,0:T(8,128)} fusion(f32[2,1,4,64,512]{4,3,2,1,0:T(8,128)S(1)} %copy-done, f32[2,4,64,512]{3,2,1,0:T(8,128)} %adjoint_gradient.1, f32[2,1,4,64,512]{4,3,2,1,0:T(8,128)S(1)} %copy-done.1), kind=kLoop, calls=%fused_computation.1 | loop fusion | flops 524288 | bytes 4194304 | tf_op jit(solution)/shard_map/reshape | solution.py:713
Async XLA Ops:
  1.3 117.7 %copy-start = (f32[2,1,4,64,512]{4,3,2,1,0:T(8,128)S(1)}, f32[2,1,4,64,512]{4,3,2,1,0:T(8,128)}, u32[]{:S(2)}) copy-start(f32[2,1,4,64,512]{4,3,2,1,0:T(8,128)} %param.27) | copy-start | bytes 3145732
  1.3 117.7 %copy-start.1 = (f32[2,1,4,64,512]{4,3,2,1,0:T(8,128)S(1)}, f32[2,1,4,64,512]{4,3,2,1,0:T(8,128)}, u32[]{:S(2)}) copy-start(f32[2,1,4,64,512]{4,3,2,1,0:T(8,128)} %param.26) | copy-start | bytes 3145732

commit v5 on v4

--- a/solution.py
+++ b/solution.py
@@ -369,7 +369,7 @@
                 m_flat[pl.ds((HALO + 8 * g) * ROWS + 8 + xp + 2 * k, 8, stride=ROWS), :] = slab[xp, 8 * g : 8 * g + 8]
         return c
 
-    lax.fori_loop(0, 16, place, 0)
+    lax.fori_loop(0, 16, place, 0, unroll=4)
     model_halo = halo(m_x, 8, land_m, hm_s, hm_r)
     model_halo[0]()
 
@@ -551,13 +551,13 @@
                 g_1[h, k, pl.ds(8 * g, 8), :] = g_flat[pl.ds((4 + 8 * g) * 32 + h + 2 * k, 8, stride=32), :]
             return c
 
-        lax.fori_loop(0, 16, gather, 0)
+        lax.fori_loop(0, 16, gather, 0, unroll=4)
 
         def turn(col, c, h=h):
             g_send[h, col] = g_1[h, (col - base_x) & 15]
             return c
 
-        lax.fori_loop(0, 16, turn, 0)
+        lax.fori_loop(0, 16, turn, 0, unroll=4)
         gd.append(
             over_dom(
                 lambda p, h=h: g_send.at[h, p],

time: 122 us -> 121 us (level)
  no operation moved by 1% of the time
where the time goes in v5:
time: 121 us
  Pallas kernels  117 us (97%)
  other arithmetic  2.54 us (2%)
  between operations  1.34 us (1%)
    pallas_call x1, Pallas kernels, local(): pl.pallas_call(kernel, out_shape=jax.ShapeDtypeStruct(shape, F32), in_spe...  117 us
    reshape x1, other arithmetic, local(): return result.reshape(velocity.shape)  2.54 us

profile of v5, /device:TPU:0, one launch (start us, length us, event | category | flops | bytes accessed | tf_op | source)
XLA Modules:
  0.0 121.1 jit_solution(2001263463679836808)
XLA Ops:
  1.3 0.0 copy-start
  1.3 0.0 copy-start.1
  1.3 117.2 %adjoint_gradient.1 = f32[2,4,64,512]{3,2,1,0:T(8,128)} custom-call(f32[2,4,64,512]{3,2,1,0:T(8,128)} %bitcast.19, f32[4,64,512]{2,1,0:T(8,128)} %bitcast.20, f32[4,64,512]{2,1,0:T(8,128)} %bitcast.21, f32[4,64,512]{2,1,0:T(8,128)} %bitcast.22, f32[4,64,512]{2,1,0:T(8,128)} %bitcast.23, s32[1,256]{1,0:T(1,128)} %rec_pos.1, f32[8,256]{1,0:T(8,128)} %bitcast.24, ...), custom_call_target="tpu_custom_call" | custom-call | tf_op jit(solution)/shard_map/adjoint_gradient/pallas_call | solution.py:690
  118.5 0.0 copy-done
  118.6 0.0 copy-done.1
  118.6 2.5 %fusion = f32[2,1,4,64,512]{4,3,2,1,0:T(8,128)} fusion(f32[2,1,4,64,512]{4,3,2,1,0:T(8,128)S(1)} %copy-done, f32[2,4,64,512]{3,2,1,0:T(8,128)} %adjoint_gradient.1, f32[2,1,4,64,512]{4,3,2,1,0:T(8,128)S(1)} %copy-done.1), kind=kLoop, calls=%fused_computation.1 | loop fusion | flops 524288 | bytes 4194304 | tf_op jit(solution)/shard_map/reshape | solution.py:713
Async XLA Ops:
  1.3 117.3 %copy-start = (f32[2,1,4,64,512]{4,3,2,1,0:T(8,128)S(1)}, f32[2,1,4,64,512]{4,3,2,1,0:T(8,128)}, u32[]{:S(2)}) copy-start(f32[2,1,4,64,512]{4,3,2,1,0:T(8,128)} %param.27) | copy-start | bytes 3145732
  1.3 117.3 %copy-start.1 = (f32[2,1,4,64,512]{4,3,2,1,0:T(8,128)S(1)}, f32[2,1,4,64,512]{4,3,2,1,0:T(8,128)}, u32[]{:S(2)}) copy-start(f32[2,1,4,64,512]{4,3,2,1,0:T(8,128)} %param.26) | copy-start | bytes 3145732
